TPU v7x, 32 devices: a whole 2x2x4 slice. The times are simulated.
32 devices in a mesh: seq: 32 (over z, y, x, core).
Axes of the slice: x: 2, y: 2, z: 4, core: 2. Of those that a mesh axis runs over, the one named last changes fastest.
Arguments:
- features: float32 [16384, 512], P('seq'), may hold values from -6 to 6
- preacts: float32 [3, 16384, 512], P(None, 'seq'), may hold values from -6 to 6
- teacher: float32 [3, 16384, 512], P(None, 'seq'), may hold values from -6 to 6
- cotangent: float32 [16384, 512], P('seq'), may hold values from -6 to 6
- kernels: float32 [3, 3, 512, 512], replicated, may hold values from -0.15625 to 0.15625
Outputs:
- input_grad: float32 [16384, 512], P('seq')
- kernel_grad: float32 [3, 3, 512, 512], P(None, None, 'seq')
All inputs are finite; a program needn't handle non-finite values.
Results may differ from a plain program's by a relative error of at most 0.0001.
Values sent between devices are 32-bit elements; how exact they have to be, the bound alone decides.
No kernel may reach another device: no remote copies, remote signals or barrier semaphores. Data moves between devices by JAX's collectives and lax.ppermute only.
A program may use at most 128 MiB of HBM per device.

v0:
```python
import math

import jax
import jax.numpy as jnp
from jax import lax
from jax.sharding import PartitionSpec as P

BASE_SPACING = 512
LAYERS = 3


mimic_weight = 0.5


def shifted(array, axis, by):
    devices = lax.axis_size(axis)
    pairs = [(i, i + by) for i in range(devices) if 0 <= i + by < devices]
    return lax.ppermute(array, axis, pairs)


def gelu_response(linear_response):
    cdf = 0.5 * (1.0 + jax.scipy.special.erf(linear_response / math.sqrt(2.0)))
    return linear_response * cdf


def gelu_slope(linear_response):
    cdf = 0.5 * (1.0 + jax.scipy.special.erf(linear_response / math.sqrt(2.0)))
    density = jnp.exp(-0.5 * linear_response * linear_response) / math.sqrt(2.0 * math.pi)
    return cdf + linear_response * density


def matmul(left, right):
    return jnp.dot(left, right, precision=lax.Precision.HIGHEST, preferred_element_type=jnp.float32)


def inner(left, right):
    return lax.dot_general(
        left,
        right,
        (((0,), (0,)), ((), ())),
        precision=lax.Precision.HIGHEST,
        preferred_element_type=jnp.float32,
    )


def shards(features, preacts, teacher, cotangent, kernels):
    resident_bins = features.shape[0]
    devices = lax.axis_size("seq")
    scale = 1.0 / math.sqrt(resident_bins * devices)
    states = [features]
    state = features
    for layer_number in range(LAYERS):
        state = state + gelu_response(preacts[layer_number])
        states.append(state)
    grad = cotangent
    layer_gradient_list = [None] * LAYERS
    for layer_number in range(LAYERS - 1, -1, -1):
        neighbor_jumps = BASE_SPACING * 2**layer_number // resident_bins
        grad = grad + mimic_weight * (states[layer_number + 1] - teacher[layer_number])
        pre_grad = grad * gelu_slope(preacts[layer_number])
        grad_prev = shifted(pre_grad, "seq", neighbor_jumps)
        grad_next = shifted(pre_grad, "seq", -neighbor_jumps)
        weights = kernels[layer_number]
        grad = (
            grad
            + matmul(grad_next, weights[0].T)
            + matmul(pre_grad, weights[1].T)
            + matmul(grad_prev, weights[2].T)
        )
        source = states[layer_number]
        terms = (
            jnp.stack([inner(source, grad_next), inner(source, pre_grad), inner(source, grad_prev)])
            * scale
        )
        layer_gradient_list[layer_number] = lax.psum_scatter(
            terms, "seq", scatter_dimension=1, tiled=True
        )
    kernel_grad = jnp.stack(layer_gradient_list)
    return (grad, kernel_grad)


def solution(mesh):
    in_specs = (P("seq", None), P(None, "seq", None), P(None, "seq", None), P("seq", None), P())
    out_specs = (P("seq", None), P(None, None, "seq", None))
    return jax.shard_map(shards, mesh=mesh, in_specs=in_specs, out_specs=out_specs, check_vma=False)
```

profile of v0, /device:TPU:0, one launch (start us, length us, event | category | flops | bytes accessed | tf_op | source)
XLA Modules:
  0.0 401.4 jit_solution(1748746218017891110)
XLA Ops:
  7.2 0.0 all-reduce.6.cloned.1.call-start
  7.2 0.0 copy-start.1
  7.2 3.5 fusion.9
  10.7 1.6 collective-permute-start
  12.2 5.6 %collective-permute-start.1 = (f32[512,512]{1,0:T(8,128)S(1)}, f32[512,512]{1,0:T(8,128)S(1)}, u32[]{:S(2)}, u32[]{:S(2)}) collective-permute-start(f32[512,512]{1,0:T(8,128)S(1)} %get-tuple-element.7), channel_id=1, source_target_pairs={{0,4},{1,5},{2,6},{3,7},{4,8},{5,9},{6,10},{7,11},{8,12},{9,13},{1... | collective-permute-start | bytes 3145736 | tf_op jit(solution)/shard_map/ppermute | solution.py:18
  17.8 0.0 copy-done.1
  17.8 0.0 copy-start.12
  17.8 1.9 fusion.31
  19.7 0.0 copy-start.4
  19.7 19.2 %collective-permute-done = f32[512,512]{1,0:T(8,128)S(1)} collective-permute-done((f32[512,512]{1,0:T(8,128)S(1)}, f32[512,512]{1,0:T(8,128)S(1)}, u32[]{:S(2)}, u32[]{:S(2)}) %collective-permute-start) | collective-permute-done | bytes 1048608 | tf_op jit(solution)/shard_map/ppermute | solution.py:18
  39.0 2.0 fusion.4
  40.9 20.7 %collective-permute-done.1 = f32[512,512]{1,0:T(8,128)S(1)} collective-permute-done((f32[512,512]{1,0:T(8,128)S(1)}, f32[512,512]{1,0:T(8,128)S(1)}, u32[]{:S(2)}, u32[]{:S(2)}) %collective-permute-start.1) | collective-permute-done | bytes 1048608 | tf_op jit(solution)/shard_map/ppermute | solution.py:18
  61.6 0.0 copy-done.12
  61.6 0.0 copy-done.4
  61.6 2.3 fusion.14
  63.9 1.3 collective-permute-start.2
  65.2 1.9 convolution_bitcast_fusion.1
  67.1 4.8 %collective-permute-start.3 = (f32[512,512]{1,0:T(8,128)S(1)}, f32[512,512]{1,0:T(8,128)S(1)}, u32[]{:S(2)}, u32[]{:S(2)}) collective-permute-start(f32[512,512]{1,0:T(8,128)S(1)} %get-tuple-element.11), channel_id=1, source_target_pairs={{0,2},{1,3},{2,4},{3,5},{4,6},{5,7},{6,8},{7,9},{8,10},{9,11},{10,... | collective-permute-start | bytes 3145736 | tf_op jit(solution)/shard_map/ppermute | solution.py:18
  71.9 3.0 convolution_bitcast_fusion.4
  74.9 1.9 convolution_bitcast_fusion
  76.9 1.9 fusion.26
  78.7 13.0 %collective-permute-done.2 = f32[512,512]{1,0:T(8,128)S(1)} collective-permute-done((f32[512,512]{1,0:T(8,128)S(1)}, f32[512,512]{1,0:T(8,128)S(1)}, u32[]{:S(2)}, u32[]{:S(2)}) %collective-permute-start.2) | collective-permute-done | bytes 1048608 | tf_op jit(solution)/shard_map/ppermute | solution.py:18
  91.8 0.0 copy-start.7
  91.8 1.9 fusion.2
  93.7 0.0 copy-done.7
  93.7 21.5 %collective-permute-done.3 = f32[512,512]{1,0:T(8,128)S(1)} collective-permute-done((f32[512,512]{1,0:T(8,128)S(1)}, f32[512,512]{1,0:T(8,128)S(1)}, u32[]{:S(2)}, u32[]{:S(2)}) %collective-permute-start.3) | collective-permute-done | bytes 1048608 | tf_op jit(solution)/shard_map/ppermute | solution.py:18
  115.1 3.2 fusion.19
  118.4 0.0 copy-done.11
  118.4 3.0 collective-permute-start.5
  121.4 1.9 convolution_bitcast_fusion.2
  123.3 1.5 collective-permute-start.4
  124.9 2.0 maximum_multiply_fusion.2
  126.9 5.1 %copy.22 = f32[3,512,512]{2,0,1:T(4,128)} copy(f32[3,512,512]{1,2,0:T(8,128)} %maximum_multiply_fusion.2) | data formatting | bytes 6291456 | tf_op jit(solution)/shard_map/mul | solution.py:72
  132.0 3.2 convolution_bitcast_fusion.3
  135.2 0.0 copy-done.8
  135.2 1.9 convolution_bitcast_fusion.5
  137.1 0.0 copy-done.9
  137.1 2.1 maximum_multiply_fusion.1
  139.2 5.3 %copy.18 = f32[3,512,512]{2,0,1:T(4,128)} copy(f32[3,512,512]{1,2,0:T(8,128)} %maximum_multiply_fusion.1) | data formatting | bytes 6291456 | tf_op jit(solution)/shard_map/mul | solution.py:72
  144.5 0.0 copy-done.2
  144.5 0.0 copy-done
  144.5 1.8 convolution_bitcast_fusion.7
  146.3 0.0 collective-permute-done.5
  146.3 3.1 convolution_bitcast_fusion.6
  149.4 0.0 collective-permute-done.4
  149.4 0.0 copy-start.5
  149.5 1.0 copy-done.5
  150.4 1.8 convolution_bitcast_fusion.8
  152.3 0.4 maximum_multiply_fusion
  152.7 3.8 copy.14
  156.5 0.0 copy-start.3
  156.5 0.0 all-reduce.6.cloned.1.call-update
  156.5 0.0 copy-start.6
  156.5 0.0 copy-start.10
  156.6 1.2 copy-done.3
  157.7 3.1 fusion.21
  160.8 0.0 copy-done.6
  160.8 0.0 copy-done.10
  160.8 3.1 fusion
  164.0 5.0 %convolution_add_fusion = f32[512,512]{1,0:T(8,128)} fusion(f32[512,512]{1,0:T(8,128)S(1)} %fusion, f32[512,512]{1,0:T(8,128)} %collective-permute-done.5, f32[3,3,512,512]{3,2,1,0:T(8,128)} %param.9), kind=kOutput, calls=%fused_computation.15 | convolution fusion | flops 1610874880 | bytes 4194304 | tf_op jit(solution)/shard_map/dot_general | solution.py:33
  169.0 222.4 %all-reduce.6.cloned.1.call-done = (f32[3,512,512]{2,0,1:T(4,128)}, f32[3,512,512]{2,0,1:T(4,128)}, f32[3,512,512]{2,0,1:T(4,128)}) async-done(((f32[3,512,512]{2,0,1:T(4,128)}, f32[3,512,512]{2,0,1:T(4,128)}, f32[3,512,512]{2,0,1:T(4,128)}), (f32[3,512,512]{2,0,1:T(4,128)}, f32[3,512,512]{2,0,1:T(4,128)}, f32[3,512,512]{2,0,1:T(4,128)})) %all-reduce.6.cloned.1.call-update) | async-done | bytes 9437200
  391.3 1.0 dynamic-slice_bitcast_fusion
  392.4 0.9 dynamic-slice_bitcast_fusion.2
  393.4 0.7 pad_maximum_fusion
  (8 shorter events, 0.1 us)
Async XLA Ops:
  7.2 384.2 %all-reduce.6.cloned.1.call-start = ((), (), s32[]{:S(2)}) async-start(), calls=%async_computation | async-start | bytes 25165824
  7.2 10.6 %copy-start.1 = (f32[3,3,512,512]{3,2,1,0:T(8,128)S(1)}, f32[3,3,512,512]{3,2,1,0:T(8,128)}, u32[]{:S(2)}) copy-start(f32[3,3,512,512]{3,2,1,0:T(8,128)} %param.9) | copy-start | bytes 28311556
  10.7 28.3 %collective-permute-start = (f32[512,512]{1,0:T(8,128)S(1)}, f32[512,512]{1,0:T(8,128)S(1)}, u32[]{:S(2)}, u32[]{:S(2)}) collective-permute-start(f32[512,512]{1,0:T(8,128)S(1)} %get-tuple-element.7), channel_id=1, source_target_pairs={{4,0},{5,1},{6,2},{7,3},{8,4},{9,5},{10,6},{11,7},{12,8},{13,9},{1... | collective-permute-start | bytes 3145736 | tf_op jit(solution)/shard_map/ppermute | solution.py:18
  12.2 49.3 %collective-permute-start.1 = (f32[512,512]{1,0:T(8,128)S(1)}, f32[512,512]{1,0:T(8,128)S(1)}, u32[]{:S(2)}, u32[]{:S(2)}) collective-permute-start(f32[512,512]{1,0:T(8,128)S(1)} %get-tuple-element.7), channel_id=1, source_target_pairs={{0,4},{1,5},{2,6},{3,7},{4,8},{5,9},{6,10},{7,11},{8,12},{9,13},{1... | collective-permute-start | bytes 3145736 | tf_op jit(solution)/shard_map/ppermute | solution.py:18
  17.8 43.8 %copy-start.12 = (f32[3,512,512]{2,1,0:T(8,128)S(1)}, f32[3,512,512]{2,1,0:T(8,128)}, u32[]{:S(2)}) copy-start(f32[3,512,512]{2,1,0:T(8,128)} %param.7) | copy-start | bytes 9437188
  19.7 41.9 %copy-start.4 = (f32[3,512,512]{2,1,0:T(8,128)S(1)}, f32[3,512,512]{2,1,0:T(8,128)}, u32[]{:S(2)}) copy-start(f32[3,512,512]{2,1,0:T(8,128)} %param.6) | copy-start | bytes 9437188
  63.9 27.9 %collective-permute-start.2 = (f32[512,512]{1,0:T(8,128)S(1)}, f32[512,512]{1,0:T(8,128)S(1)}, u32[]{:S(2)}, u32[]{:S(2)}) collective-permute-start(f32[512,512]{1,0:T(8,128)S(1)} %get-tuple-element.11), channel_id=1, source_target_pairs={{2,0},{3,1},{4,2},{5,3},{6,4},{7,5},{8,6},{9,7},{10,8},{11,9},{12,... | collective-permute-start | bytes 3145736 | tf_op jit(solution)/shard_map/ppermute | solution.py:18
  67.1 48.0 %collective-permute-start.3 = (f32[512,512]{1,0:T(8,128)S(1)}, f32[512,512]{1,0:T(8,128)S(1)}, u32[]{:S(2)}, u32[]{:S(2)}) collective-permute-start(f32[512,512]{1,0:T(8,128)S(1)} %get-tuple-element.11), channel_id=1, source_target_pairs={{0,2},{1,3},{2,4},{3,5},{4,6},{5,7},{6,8},{7,9},{8,10},{9,11},{10,... | collective-permute-start | bytes 3145736 | tf_op jit(solution)/shard_map/ppermute | solution.py:18
  91.8 1.9 copy-start.7
  115.1 3.3 copy-start.11
  118.4 26.1 %copy-start.2 = (f32[512,512]{1,0:T(8,128)}, f32[512,512]{1,0:T(8,128)S(1)}, u32[]{:S(2)}) copy-start(f32[512,512]{1,0:T(8,128)S(1)} %get-tuple-element.13) | copy-start | bytes 3145732
  118.4 27.9 %collective-permute-start.5 = (f32[512,512]{1,0:T(8,128)S(1)}, f32[512,512]{1,0:T(8,128)}, u32[]{:S(2)}, u32[]{:S(2)}) collective-permute-start(f32[512,512]{1,0:T(8,128)S(1)} %get-tuple-element.13), channel_id=1, source_target_pairs={{0,1},{1,2},{2,3},{3,4},{4,5},{5,6},{6,7},{7,8},{8,9},{9,10},{10,1... | collective-permute-start | bytes 3145736 | tf_op jit(solution)/shard_map/ppermute | solution.py:18
  123.3 26.1 %collective-permute-start.4 = (f32[512,512]{1,0:T(8,128)S(1)}, f32[512,512]{1,0:T(8,128)S(1)}, u32[]{:S(2)}, u32[]{:S(2)}) collective-permute-start(f32[512,512]{1,0:T(8,128)S(1)} %get-tuple-element.13), channel_id=1, source_target_pairs={{1,0},{2,1},{3,2},{4,3},{5,4},{6,5},{7,6},{8,7},{9,8},{10,9},{11,1... | collective-permute-start | bytes 3145736 | tf_op jit(solution)/shard_map/ppermute | solution.py:18
  132.0 3.3 copy-start.8
  132.0 5.2 %copy-start.9 = (f32[1,512,512]{1,2,0:T(8,128)S(1)}, f32[1,512,512]{1,2,0:T(8,128)}, u32[]{:S(2)}) copy-start(f32[1,512,512]{1,2,0:T(8,128)} %convolution_bitcast_fusion.4) | copy-start | bytes 3145732
  139.2 5.3 %copy-start = (f32[512,512]{1,0:T(8,128)S(1)}, f32[512,512]{1,0:T(8,128)}, u32[]{:S(2)}) copy-start(f32[512,512]{1,0:T(8,128)} %param.5) | copy-start | bytes 3145732
  149.4 1.0 copy-start.5
  156.5 1.2 copy-start.3
  156.5 4.3 %copy-start.6 = (f32[512,512]{1,0:T(8,128)S(1)}, f32[512,512]{1,0:T(8,128)}, u32[]{:S(2)}) copy-start(f32[512,512]{1,0:T(8,128)} %copy-done.5) | copy-start | bytes 3145732
  156.5 4.3 %copy-start.10 = (f32[512,512]{1,0:T(8,128)S(1)}, f32[512,512]{1,0:T(8,128)}, u32[]{:S(2)}) copy-start(f32[512,512]{1,0:T(8,128)} %get-tuple-element.14) | copy-start | bytes 3145732
Sparse Core Ops, SparseCore 0:
  156.6 234.6 all-reduce.5
where the time goes:
time: 409 us; the launch traced here: 401 us
  waiting for transfers between devices  297 us (73%)
  matrix products  45 us (11%)
  local copies, waits for them, and re-layouts  18.4 us (4%)
  starting transfers between devices  17.7 us (4%)
  between operations  14.8 us (4%)
  other arithmetic  8.65 us (2%)
    unnamed x2, waiting for transfers between devices  222 us
    ppermute x6, waiting for transfers between devices, shifted(): return lax.ppermute(array, axis, pairs)  74.4 us
    dot_general x9, matrix products, matmul(): jnp.dot(left, right, precision=lax.Precision.HIGHEST, preferred_element_t...  24.3 us
    dot_general x9, matrix products, inner(): lax.dot_general(left, right, (((0,), (0,)), ((), ())), precision=lax.Prec...  20.7 us
    ppermute x6, starting transfers between devices, shifted(): return lax.ppermute(array, axis, pairs)  17.7 us
    mul x3, local copies, waits for them, and re-layouts, shards(): jnp.stack([inner(source, grad_next), inner(source, pre_grad), inner(sourc...  14.2 us
  transfers between devices with their start and end apart: 7, of which 5 were waited for; matrix products, arithmetic and copies ran while one was open for 13% of the time, Pallas kernels for 0%

commit v1 on v0

v1 whole, which is shorter than its diff:
```python
import math

import jax
import jax.numpy as jnp
from jax import lax
from jax.experimental import pallas as pl
from jax.experimental.pallas import tpu as pltpu
from jax.sharding import PartitionSpec as P

BASE_SPACING = 512
LAYERS = 3
MIMIC_WEIGHT = 0.5
F32 = jnp.float32
STRIP = 32
PIECES = (2,)
GROUPS = (((0,), (1, 3), (2, 4)), ((0,), (2,), (4,), (3,), (1,)), ((0,), (2,), (4,), (3,), (1,)))
FIRST_SIXTEENTHS = 8
UNIT = 5 * 10**9
ORDER = (
    ("top", 0), ("prep", 0), ("turn", 0), ("w2", 0), ("ca2", 0), ("aa2", 0),
    ("w1", 0), ("cb2", 0), ("ca1", 0), ("m2", 0), ("ab2", 0), ("t2", 0), ("aa1", 0),
    ("w0", 0), ("cb1", 0), ("ca0", 0), ("m1", 0), ("ab1", 4), ("r2", 0), ("aa0", 0),
    ("t1", 0), ("m0", 0), ("cb0", 0),
    ("ab0", 0), ("t0", 0), ("r1", 0), ("r2", 0), ("r0", 0), ("r2", 0), ("r1", 0),
    ("r0", 0), ("r1", 0), ("r2", 0), ("r1", 0),
)


def paired(array, jump, parity):
    devices = lax.axis_size("seq")
    pairs = []
    for i in range(devices):
        j = i + jump if (i // jump) % 2 == parity else i - jump
        if 0 <= j < devices:
            pairs.append((i, j))
    return lax.ppermute(array, "seq", pairs)


def swapped(array, mask):
    devices = lax.axis_size("seq")
    return lax.ppermute(array, "seq", [(i, i ^ mask) for i in range(devices)])


def gelu_and_slope(u):
    cdf = 0.5 * (1.0 + lax.erf(u * math.sqrt(0.5)))
    density = jnp.exp(-0.5 * u * u) * (1.0 / math.sqrt(2.0 * math.pi))
    return u * cdf, cdf + u * density


def dot(left, right, precision=lax.Precision.HIGH):
    return jnp.dot(left, right, precision=precision, preferred_element_type=F32)


def dot_nt(left, right, precision=lax.Precision.HIGH):
    return lax.dot_general(
        left, right, (((1,), (1,)), ((), ())), precision=precision, preferred_element_type=F32
    )


class Line:
    def __init__(self, scalars):
        self.last = None
        self.scalars = scalars

    def __call__(self, body, inputs, outputs, limit=24, work=0):
        arrays, specs = [], []
        for item in inputs:
            array, spec = item if isinstance(item, tuple) else (item, None)
            arrays.append(array)
            specs.append(spec or pl.BlockSpec(array.shape, lambda i, s, n=array.ndim: (0,) * n))
        count = len(arrays)
        if self.last is not None:
            arrays.append(self.last)
            specs.append(pl.BlockSpec(memory_space=pl.ANY))
        total = len(arrays)

        def kernel(scalars, *refs):
            body(scalars, *refs[:count], *refs[total:])

        out = pl.pallas_call(
            kernel,
            grid_spec=pltpu.PrefetchScalarGridSpec(
                num_scalar_prefetch=1,
                grid=(1,),
                in_specs=specs,
                out_specs=[pl.BlockSpec(s, lambda i, _, n=len(s): (0,) * n) for s in outputs],
            ),
            out_shape=[jax.ShapeDtypeStruct(s, F32) for s in outputs],
            compiler_params=pltpu.CompilerParams(vmem_limit_bytes=limit * 2**20),
            cost_estimate=pl.CostEstimate(flops=work * UNIT, bytes_accessed=1024, transcendentals=0),
        )(self.scalars, *arrays)
        self.last = out[0]
        return out


class Scatter:
    def __init__(self, line, groups):
        self.line, self.groups, self.keep, self.received = line, list(groups), [], []
        (self.first,) = self.groups.pop(0)

    def add(self, send, keep):
        self.keep.append(keep)
        self.received.append([(0, swapped(send, 1 << self.first))])

    def step(self, work):
        bits = self.groups.pop(0)
        parts = 1 << len(bits)
        keeps, received = self.keep, self.received
        rows = keeps[0].shape[0] // parts
        columns = sum(k.shape[1] for k in keeps)
        flat = [array for group in received for _, array in group]
        count = len(keeps)

        def body(_, *refs):
            got, outs = refs[count : count + len(flat)], refs[count + len(flat) :]
            for q, out_ref in enumerate(outs):
                r = slice(q * rows, (q + 1) * rows)
                at = n = 0
                for keep_ref, group in zip(refs[:count], received):
                    value = keep_ref[r, :]
                    for _ in group:
                        value = value + got[n][r, :]
                        n += 1
                    out_ref[:, at : at + keep_ref.shape[1]] = value
                    at += keep_ref.shape[1]

        keep, *sends = self.line(body, [*keeps, *flat], [(rows, columns)] * parts, work=work)
        group = []
        for q, send in enumerate(sends, 1):
            mask = sum(1 << bit for n, bit in enumerate(reversed(bits)) if (q >> n) & 1)
            group.append((q, swapped(send, mask)))
        self.keep, self.received = [keep], [group]

    def result(self):
        assert not self.groups
        return sum((array for _, array in self.received[0]), self.keep[0])


def shards(features, preacts, teacher, cotangent, kernels):
    bins, channels = features.shape
    devices = lax.axis_size("seq")
    width = devices.bit_length() - 1
    me = lax.axis_index("seq")
    scale = 1.0 / math.sqrt(bins * devices)
    jumps = [BASE_SPACING * 2**layer // bins for layer in range(LAYERS)]
    groups = []
    for layer in GROUPS:
        known = [g for g in (tuple(b for b in bits if b < width) for bits in layer) if g]
        listed = [b for g in known for b in g]
        groups.append(known + [(b,) for b in range(width) if b not in listed])
    parity = jnp.stack([(me // jump) % 2 for jump in jumps]).astype(jnp.int32)
    cut = FIRST_SIXTEENTHS * bins // 16
    spans = ((0, cut), (cut, bins))
    line = Line(parity)
    full = (bins, channels)
    square = (channels, channels)
    parts = [(stop - start, channels) for start, stop in spans]

    def rows_of(array, c, lead=None):
        start, stop = spans[c]
        if lead is None:
            block = (pl.Element(stop - start), pl.Element(channels))
            return array, pl.BlockSpec(block, lambda i, s: (start, 0))
        block = (pl.Squeezed(), pl.Element(stop - start), pl.Element(channels))
        return array, pl.BlockSpec(block, lambda i, s: (lead, start, 0))

    def halo(gu, layer):
        return paired(gu, jumps[layer], 0), paired(gu, jumps[layer], 1)

    def strips(rows):
        return pl.loop(0, rows // STRIP)

    def strip(i):
        return pl.ds(pl.multiple_of(i * STRIP, STRIP), STRIP)

    def top():
        def body(_, x_ref, u0_ref, u1_ref, u2_ref, t_ref, cot_ref, g_ref, gu_ref):
            @strips(cut)
            def _(i):
                r = strip(i)
                x = x_ref[r, :] + gelu_and_slope(u0_ref[r, :])[0]
                x = x + gelu_and_slope(u1_ref[r, :])[0]
                response, slope = gelu_and_slope(u2_ref[r, :])
                g = cot_ref[r, :] + MIMIC_WEIGHT * (x + response - t_ref[r, :])
                g_ref[r, :] = g
                gu_ref[r, :] = g * slope

        ins = [rows_of(features, 0), *(rows_of(preacts, 0, l) for l in range(LAYERS))]
        ins += [rows_of(teacher, 0, 2), rows_of(cotangent, 0)]
        return line(body, ins, [parts[0]] * 2, 63)

    def prepare():
        def body(_, x_ref, u_ref, t_ref, cot_ref, *refs):
            x1_ref, x2_ref, *pairs, g_ref, gu_ref = refs

            def both(i, c):
                r = strip(i + spans[c][0] // STRIP)
                low = strip(i)
                h0_ref, s0_ref, h1_ref, s1_ref = pairs[4 * c : 4 * c + 4]
                response, s0_ref[low, :] = gelu_and_slope(u_ref[0, r, :])
                x1 = x_ref[r, :] + response
                x1_ref[r, :] = x1
                h0_ref[low, :] = MIMIC_WEIGHT * (x1 - t_ref[0, r, :])
                response, s1_ref[low, :] = gelu_and_slope(u_ref[1, r, :])
                x2 = x1 + response
                x2_ref[r, :] = x2
                h1_ref[low, :] = MIMIC_WEIGHT * (x2 - t_ref[1, r, :])
                return r, low, x2

            @strips(cut)
            def _(i):
                both(i, 0)

            @strips(bins - cut)
            def _(i):
                r, low, x2 = both(i, 1)
                response, slope = gelu_and_slope(u_ref[2, r, :])
                g = cot_ref[r, :] + MIMIC_WEIGHT * (x2 + response - t_ref[2, r, :])
                g_ref[low, :] = g
                gu_ref[low, :] = g * slope

        ins = [features, preacts, teacher, cotangent]
        return line(body, ins, [full] * 2 + [parts[0]] * 4 + [parts[1]] * 6, 56)

    def weights(layer):
        def body(_, *refs):
            for source, target in zip(refs[:3], refs[3:]):
                target[...] = source[...]

        block = (pl.Squeezed(), pl.Squeezed(), channels, channels)
        ins = [
            (kernels, pl.BlockSpec(block, lambda i, s: (layer, 2 * s[layer], 0, 0))),
            (kernels, pl.BlockSpec(block, lambda i, s: (layer, 1, 0, 0))),
            (kernels, pl.BlockSpec(block, lambda i, s: (layer, 2 - 2 * s[layer], 0, 0))),
        ]
        return line(body, ins, [square] * 3)

    def turn(xs):
        block = channels // devices
        sources = []
        for layer in range(LAYERS):
            row = jnp.arange(channels, dtype=jnp.int32)
            index = row // block
            target = jnp.zeros_like(row)
            for place, bit in enumerate(b for g in groups[layer] for b in g):
                target = target | (((index >> (width - 1 - place)) & 1) << bit)
            sources.append((target ^ me) * block + row % block)
        sources = jnp.stack(sources)[:, :, None]

        def body(_, source_ref, *refs):
            lanes = lax.broadcasted_iota(jnp.int32, (channels, channels), 1)
            for l in range(LAYERS):
                pick = jnp.where(lanes == source_ref[l], 1.0, 0.0)
                refs[LAYERS + l][...] = dot_nt(pick, refs[l][...])

        return line(body, [sources, *xs], [(channels, bins)] * LAYERS)

    def center(g, gu, w, carried=None):
        carry = [] if carried is None else [carried]

        def body(_, g_ref, gu_ref, w_ref, *refs):
            refs[len(carry)][...] = g_ref[...] + dot_nt(gu_ref[...], w_ref[...])
            if carry:
                refs[2][...] = refs[0][...]

        return line(body, [g, gu, w, *carry], [g.shape] + [c.shape for c in carry])

    def advance(base, sides, wp, wq, pull=None, slope=None, work=0):
        def body(_, base_ref, p_ref, q_ref, wp_ref, wq_ref, *refs):
            g = base_ref[...] + dot_nt(p_ref[...], wp_ref[...])
            g = g + dot_nt(q_ref[...], wq_ref[...])
            if pull is None:
                refs[0][...] = g
            else:
                pull_ref, slope_ref, g_ref, gu_ref = refs
                g = g + pull_ref[...]
                g_ref[...] = g
                gu_ref[...] = g * slope_ref[...]

        ins = [base, *sides, wp, wq]
        if pull is None:
            return line(body, ins, [base.shape], work=work)
        return line(body, ins + [pull, slope], [base.shape] * 2, work=work)

    rows = channels // 2

    def middle(layer, x, gu_a, gu_b, work):
        def body(_, x_ref, a_ref, b_ref, *outs):
            both = jnp.concatenate([a_ref[...], b_ref[...]], axis=0)
            value = dot(x_ref[...], both)
            for n, out_ref in enumerate(outs):
                out_ref[...] = value[rows * n : rows * (n + 1), :]

        keep, send = line(body, [x, gu_a, gu_b], [(rows, channels)] * 2, work=work)
        sums[layer].add(send, keep)

    def terms(layer, x, sides_a, sides_b, work):
        def body(s_ref, x_ref, *refs):
            for k in range(2):
                column = s_ref[layer] if k == 0 else 1 - s_ref[layer]
                place = pl.ds(pl.multiple_of(column * channels, channels), channels)
                both = jnp.concatenate([refs[k][...], refs[2 + k][...]], axis=0)
                value = dot(x_ref[...], both)
                for n, out_ref in enumerate(refs[4:]):
                    out_ref[:, place] = value[rows * n : rows * (n + 1), :]

        shapes = [(rows, 2 * channels)] * 2
        keep, send = line(body, [x, *sides_a, *sides_b], shapes, work=work)
        sums[layer].add(send, keep)

    sums = [Scatter(line, groups[layer]) for layer in range(LAYERS)]
    w, base, g, gu, halos = {}, {}, {}, {}, {}
    pull, slope = {}, {}
    for name, work in ORDER:
        kind, layer = name[:-1], int(name[-1]) if name[-1].isdigit() else None
        if name == "top":
            g["a"], gu["a", 2] = top()
            halos["a", 2] = halo(gu["a", 2], 2)
        elif name == "prep":
            x1, x2, *pairs, g["b"], carried = prepare()
            for c, key in enumerate("ab"):
                h = pairs[4 * c : 4 * c + 4]
                pull[key, 1], slope[key, 1], pull[key, 2], slope[key, 2] = h
        elif name == "turn":
            xt = turn((features, x1, x2))
        elif kind == "w":
            w[layer] = weights(layer)
        elif name == "ca2":
            base["a"], gu["b", 2] = center(g["a"], gu["a", 2], w[2][1], carried)
            halos["b", 2] = halo(gu["b", 2], 2)
        elif kind in ("ca", "cb"):
            key = kind[1]
            (base[key],) = center(g[key], gu[key, layer], w[layer][1])
        elif kind in ("aa", "ab"):
            key = kind[1]
            args = base[key], halos[key, layer], w[layer][0], w[layer][2]
            if layer:
                g[key], gu[key, layer - 1] = advance(
                    *args, pull[key, layer], slope[key, layer], work=work
                )
                halos[key, layer - 1] = halo(gu[key, layer - 1], layer - 1)
            else:
                (g[key],) = advance(*args, work=work)
        elif kind == "m":
            middle(layer, xt[layer], gu["a", layer], gu["b", layer], work)
        elif kind == "t":
            terms(layer, xt[layer], halos["a", layer], halos["b", layer], work)
        else:
            sums[layer].step(work)
    for s in sums:
        while s.groups:
            s.step(0)
    done = [s.result() for s in sums]
    grads = jnp.stack(done) * scale
    grads = grads.reshape(LAYERS, channels // devices, 3, channels).transpose(0, 2, 1, 3)
    grads = jnp.stack([grads[:, 1], grads[:, 0], grads[:, 2]], axis=1)
    return jnp.concatenate([g["a"], g["b"]], axis=0), grads


def solution(mesh):
    in_specs = (P("seq", None), P(None, "seq", None), P(None, "seq", None), P("seq", None), P())
    out_specs = (P("seq", None), P(None, None, "seq", None))
    return jax.shard_map(shards, mesh=mesh, in_specs=in_specs, out_specs=out_specs, check_vma=False)
```

time: 409 us -> 199 us (0.49); the launches traced: 401 us -> 199 us
  waiting for transfers between devices: 297 us -> 68.6 us
  Pallas kernels: 0 us -> 55.5 us
  starting transfers between devices: 17.7 us -> 62.8 us
  matrix products: 45 us -> 0 us
  between operations: 14.8 us -> 1.39 us
  local copies, waits for them, and re-layouts: 18.4 us -> 8.55 us
  other arithmetic: 8.65 us -> 2.08 us
    unnamed x2 -> x0, waiting for transfers between devices: 222 us -> none
    pallas_call x0 -> x34, Pallas kernels: none -> 55.5 us  [__call__(): pl.pallas_call(kernel, grid_spec=pltpu.PrefetchScalarGridSpec(num_scalar_...]
    ppermute x6 -> x32, starting transfers between devices: 17.7 us -> 62.8 us  [the longest x20 47.6 us: swapped(): return lax.ppermute(array, 'seq', [(i, i ^ mask) for i in range(devices)])]
    dot_general x18 -> x0, matrix products: 45 us -> none  [the longest x9 24.3 us: matmul(): jnp.dot(left, right, precision=lax.Precision.HIGHEST, preferred_element_t...]
    mul x3 -> x0, local copies, waits for them, and re-layouts: 14.2 us -> none  [shards(): jnp.stack([inner(source, grad_next), inner(source, pre_grad), inner(sourc...]
    mul x4 -> x0, other arithmetic: 7.91 us -> none  [the longest x3 4.46 us: shards(): jnp.stack([inner(source, grad_next), inner(source, pre_grad), inner(sourc...]
    ppermute x6 -> x32, waiting for transfers between devices: 74.4 us -> 68.6 us  [the longest x20 36.8 us: swapped(): return lax.ppermute(array, 'seq', [(i, i ^ mask) for i in range(devices)])]
    unnamed x26 -> x41, local copies, waits for them, and re-layouts: 2.2 us -> 7.83 us
  transfers between devices with their start and end apart: 7 -> 32, of which waited for: 5 -> 8; matrix products, arithmetic and copies ran while one was open for 13% -> 1% of each run, Pallas kernels for 0% -> 24%
where the time goes in v1:
time: 199 us
  waiting for transfers between devices  68.6 us (34%)
  starting transfers between devices  62.8 us (32%)
  Pallas kernels  55.5 us (28%)
  local copies, waits for them, and re-layouts  8.55 us (4%)
  other arithmetic  2.08 us (1%)
    pallas_call x34, Pallas kernels, __call__(): pl.pallas_call(kernel, grid_spec=pltpu.PrefetchScalarGridSpec(num_scalar_...  55.5 us
    ppermute x20, starting transfers between devices, swapped(): return lax.ppermute(array, 'seq', [(i, i ^ mask) for i in range(devices)])  47.6 us
    ppermute x20, waiting for transfers between devices, swapped(): return lax.ppermute(array, 'seq', [(i, i ^ mask) for i in range(devices)])  36.8 us
    ppermute x12, waiting for transfers between devices, paired(): return lax.ppermute(array, 'seq', pairs)  31.9 us
    ppermute x12, starting transfers between devices, paired(): return lax.ppermute(array, 'seq', pairs)  15.1 us
    unnamed x41, local copies, waits for them, and re-layouts  7.83 us
  transfers between devices with their start and end apart: 32, of which 8 were waited for; matrix products, arithmetic and copies ran while one was open for 1% of the time, Pallas kernels for 24%

profile of v1, /device:TPU:0, one launch (start us, length us, event | category | flops | bytes accessed | tf_op | source)
XLA Modules:
  0.0 198.9 jit_solution(3376279862351556851)
XLA Ops:
  1.3 4.0 %shard_map.68 = (f32[256,512]{1,0:T(8,128)}, f32[256,512]{1,0:T(8,128)}) custom-call(s32[3]{0:T(128)} %pad_add_fusion.scalars, f32[512,512]{1,0:T(8,128)} %refs_1_.8, f32[3,512,512]{2,1,0:T(8,128)} %refs_1_.7, f32[3,512,512]{2,1,0:T(8,128)} %refs_1_.7, f32[3,512,512]{2,1,0:T(8,128)} %refs_1_.7, f32[3,512,512]{2,1,0:T(8,128)} %refs_2_.6, f32[512,512]{1,0:T(8,128)} %refs_3_.3), custom_call_target="tpu_custom_call" | custom-call | bytes 1024 | tf_op jit(solution)/shard_map/pallas_call | solution.py:80
  5.3 3.0 %collective-permute-start = (f32[256,512]{1,0:T(8,128)}, f32[256,512]{1,0:T(8,128)S(1)}, u32[]{:S(2)}, u32[]{:S(2)}) collective-permute-start(f32[256,512]{1,0:T(8,128)} %get-tuple-element.75.refs_1_), channel_id=1, source_target_pairs={{0,4},{1,5},{2,6},{3,7},{4,0},{5,1},{6,2},{7,3},{8,12},{9,13},{10,... | collective-permute-start | bytes 1572872 | tf_op jit(solution)/shard_map/ppermute | solution.py:36
  8.3 1.5 collective-permute-start.1
  9.8 8.6 %shard_map.69 = (f32[512,512]{1,0:T(8,128)}, f32[512,512]{1,0:T(8,128)}, f32[256,512]{1,0:T(8,128)}, f32[256,512]{1,0:T(8,128)}, f32[256,512]{1,0:T(8,128)}, /*i...) custom-call(s32[3]{0:T(128)} %pad_add_fusion.scalars, ...), custom_call_target="tpu_custom_call" | custom-call | bytes 1024 | tf_op jit(solution)/shard_map/pallas_call | solution.py:80
  18.7 1.2 copy-done.2
  19.9 1.2 copy-done.5
  21.1 3.3 %shard_map.70 = (f32[512,512]{1,0:T(8,128)S(1)}, f32[512,512]{1,0:T(8,128)S(1)}, f32[512,512]{1,0:T(8,128)S(1)}) custom-call(s32[3]{0:T(128)S(1)} %copy-done.6, s32[3,512,1]{2,1,0:T(8,128)S(1)} %copy.10.refs_0_, f32[512,512]{1,0:T(8,128)S(1)} %copy-done.1, f32[512,512]{1,0:T(8,128)S(1)} %copy-done.2, f32[512,512]{1,0:T(8,128)S(1)} %copy-done.5, ...), custom_call_target="tpu_custom_call" | custom-call | bytes 1024 | tf_op jit(solution)/shard_map/pallas_call | solution.py:80
  24.5 3.7 %copy-done = f32[3,3,512,512]{3,2,1,0:T(8,128)S(1)} copy-done((f32[3,3,512,512]{3,2,1,0:T(8,128)S(1)}, f32[3,3,512,512]{3,2,1,0:T(8,128)}, u32[]{:S(2)}) %copy-start) | copy-done | bytes 9437208
  28.2 0.7 shard_map.71
  29.5 1.2 shard_map.72
  30.7 3.6 %collective-permute-start.4 = (f32[256,512]{1,0:T(8,128)S(1)}, f32[256,512]{1,0:T(8,128)S(1)}, u32[]{:S(2)}, u32[]{:S(2)}) collective-permute-start(f32[256,512]{1,0:T(8,128)S(1)} %get-tuple-element.90.refs_1_.refs_2_), channel_id=1, source_target_pairs={{0,4},{1,5},{2,6},{3,7},{4,0},{5,1},{6,2},{7,3},{8,12},{9,13},{10,... | collective-permute-start | bytes 1572872 | tf_op jit(solution)/shard_map/ppermute | solution.py:36
  34.3 0.7 collective-permute-start.5
  35.0 2.7 %shard_map.73 = (f32[256,512]{1,0:T(8,128)S(1)}, f32[256,512]{1,0:T(8,128)S(1)}) custom-call(s32[3]{0:T(128)S(1)} %copy-done.6, f32[256,512]{1,0:T(8,128)S(1)} %get-tuple-element.82.refs_0_.refs_7_, f32[256,512]{1,0:T(8,128)S(1)} %collective-permute-done.refs_1_, f32[256,512]{1,0:T(8,128)} %collective-permute-done.1.refs_2_, ...), custom_call_target="tpu_custom_call" | custom-call | bytes 1024 | tf_op jit(solution)/shard_map/pallas_call | solution.py:80
  37.7 1.6 collective-permute-start.2
  39.3 0.7 collective-permute-start.3
  40.0 0.7 shard_map.74
  41.0 1.2 shard_map.75.refs_3_.refs_0_
  42.2 1.2 shard_map.76.refs_3_.refs_0_
  43.4 1.6 shard_map.77
  45.0 22.3 %collective-permute-done.4.refs_1_.refs_3_ = f32[256,512]{1,0:T(8,128)S(1)} collective-permute-done((f32[256,512]{1,0:T(8,128)S(1)}, f32[256,512]{1,0:T(8,128)S(1)}, u32[]{:S(2)}, u32[]{:S(2)}) %collective-permute-start.4) | collective-permute-done | bytes 524320 | tf_op jit(solution)/shard_map/ppermute | solution.py:36
  67.4 1.6 shard_map.78
  69.0 1.6 collective-permute-start.10
  70.6 0.9 collective-permute-start.11
  71.5 3.5 %shard_map.79 = (f32[256,1024]{1,0:T(8,128)S(1)}, f32[256,1024]{1,0:T(8,128)S(1)}) custom-call(s32[3]{0:T(128)S(1)} %copy-done.6, f32[512,512]{1,0:T(8,128)S(1)} %get-tuple-element.95.refs_0_, f32[256,512]{1,0:T(8,128)S(1)} %collective-permute-done.refs_1_, f32[256,512]{1,0:T(8,128)} %collective-permute-done.1.refs_2_, ...), custom_call_target="tpu_custom_call" | custom-call | bytes 1024 | tf_op jit(solution)/shard_map/pallas_call | solution.py:80
  75.5 1.6 shard_map.80
  77.2 0.7 shard_map.81
  77.9 1.2 shard_map.82.refs_3_.refs_0_
  79.3 1.2 shard_map.83.refs_3_.refs_0_
  80.5 1.6 shard_map.84
  82.1 9.5 %collective-permute-done.10.refs_1_.refs_3_ = f32[256,512]{1,0:T(8,128)S(1)} collective-permute-done((f32[256,512]{1,0:T(8,128)S(1)}, f32[256,512]{1,0:T(8,128)S(1)}, u32[]{:S(2)}, u32[]{:S(2)}) %collective-permute-start.10) | collective-permute-done | bytes 524320 | tf_op jit(solution)/shard_map/ppermute | solution.py:36
  91.6 0.7 collective-permute-start.7
  92.3 1.6 shard_map.85
  93.9 0.7 shard_map.86
  94.7 1.6 shard_map.87.refs_5_
  96.3 2.4 %shard_map.88 = (f32[256,1024]{1,0:T(8,128)S(1)}, f32[256,1024]{1,0:T(8,128)S(1)}) custom-call(s32[3]{0:T(128)S(1)} %copy-done.6, f32[512,512]{1,0:T(8,128)S(1)} %get-tuple-element.111.refs_0_, f32[256,512]{1,0:T(8,128)S(1)} %collective-permute-done.2.refs_1_, f32[256,512]{1,0:T(8,128)S(1)} %collective-permute-done.3.refs_2_, ...), custom_call_target="tpu_custom_call" | custom-call | bytes 1024 | tf_op jit(solution)/shard_map/pallas_call | solution.py:80
  98.8 13.1 %collective-permute-start.18 = (f32[256,1024]{1,0:T(8,128)S(1)}, f32[256,1024]{1,0:T(8,128)S(1)}, u32[]{:S(2)}, u32[]{:S(2)}) collective-permute-start(f32[256,1024]{1,0:T(8,128)S(1)} %get-tuple-element.123), channel_id=1, source_target_pairs={{0,1},{1,0},{2,3},{3,2},{4,5},{5,4},{6,7},{7,6},{8,9},{9,8},{10,11... | collective-permute-start | bytes 3145736 | tf_op jit(solution)/shard_map/ppermute | solution.py:41
  112.0 0.9 collective-permute-start.13
  112.9 4.2 %collective-permute-start.17 = (f32[256,512]{1,0:T(8,128)S(1)}, f32[256,512]{1,0:T(8,128)S(1)}, u32[]{:S(2)}, u32[]{:S(2)}) collective-permute-start(f32[256,512]{1,0:T(8,128)S(1)} %get-tuple-element.122), channel_id=1, source_target_pairs={{0,1},{1,0},{2,3},{3,2},{4,5},{5,4},{6,7},{7,6},{8,9},{9,8},{10,11... | collective-permute-start | bytes 1572872 | tf_op jit(solution)/shard_map/ppermute | solution.py:41
  117.1 1.1 collective-permute-start.16
  118.2 1.6 shard_map.89
  119.8 1.2 shard_map.90.refs_0_.refs_5_
  121.0 1.6 shard_map.91.refs_5_
  122.6 2.4 %shard_map.92 = (f32[256,1024]{1,0:T(8,128)S(1)}, f32[256,1024]{1,0:T(8,128)S(1)}) custom-call(s32[3]{0:T(128)S(1)} %copy-done.6, f32[512,512]{1,0:T(8,128)S(1)} %get-tuple-element.78.refs_3_.refs_0_, f32[256,512]{1,0:T(8,128)S(1)} %collective-permute-done.6.refs_1_, f32[256,512]{1,0:T(8,128)S(1)} %collective-permute-done.7.refs_2_, ...), custom_call_target="tpu_custom_call" | custom-call | bytes 1024 | tf_op jit(solution)/shard_map/pallas_call | solution.py:80
  125.1 8.0 %collective-permute-start.15 = (f32[256,1024]{1,0:T(8,128)S(1)}, f32[256,1024]{1,0:T(8,128)S(1)}, u32[]{:S(2)}, u32[]{:S(2)}) collective-permute-start(f32[256,1024]{1,0:T(8,128)S(1)} %get-tuple-element.120), channel_id=1, source_target_pairs={{0,1},{1,0},{2,3},{3,2},{4,5},{5,4},{6,7},{7,6},{8,9},{9,8},{10,11... | collective-permute-start | bytes 3145736 | tf_op jit(solution)/shard_map/ppermute | solution.py:41
  133.1 0.7 shard_map.93
  133.9 0.9 collective-permute-start.22
  134.9 5.2 %collective-permute-done.16.refs_1_ = f32[128,1536]{1,0:T(8,128)S(1)} collective-permute-done((f32[128,1536]{1,0:T(8,128)S(1)}, f32[128,1536]{1,0:T(8,128)S(1)}, u32[]{:S(2)}, u32[]{:S(2)}) %collective-permute-start.16) | collective-permute-done | bytes 786464 | tf_op jit(solution)/shard_map/ppermute | solution.py:41
  140.8 4.7 %collective-permute-start.23 = (f32[64,1536]{1,0:T(8,128)S(1)}, f32[64,1536]{1,0:T(8,128)S(1)}, u32[]{:S(2)}, u32[]{:S(2)}) collective-permute-start(f32[64,1536]{1,0:T(8,128)S(1)} %get-tuple-element.131), channel_id=1, source_target_pairs={{0,16},{1,17},{2,18},{3,19},{4,20},{5,21},{6,22},{7,23},{8,24},{9,... | collective-permute-start | bytes 1179656 | tf_op jit(solution)/shard_map/ppermute | solution.py:41
  145.5 0.7 shard_map.95
  146.3 2.3 %collective-permute-start.20 = (f32[64,1536]{1,0:T(8,128)S(1)}, f32[64,1536]{1,0:T(8,128)S(1)}, u32[]{:S(2)}, u32[]{:S(2)}) collective-permute-start(f32[64,1536]{1,0:T(8,128)S(1)} %get-tuple-element.128), channel_id=1, source_target_pairs={{0,2},{1,3},{2,0},{3,1},{4,6},{5,7},{6,4},{7,5},{8,10},{9,11},{10,... | collective-permute-start | bytes 1179656 | tf_op jit(solution)/shard_map/ppermute | solution.py:41
  148.5 1.4 collective-permute-start.21
  149.9 12.8 %collective-permute-done.23.refs_1_ = f32[64,1536]{1,0:T(8,128)S(1)} collective-permute-done((f32[64,1536]{1,0:T(8,128)S(1)}, f32[64,1536]{1,0:T(8,128)S(1)}, u32[]{:S(2)}, u32[]{:S(2)}) %collective-permute-start.23) | collective-permute-done | bytes 393248 | tf_op jit(solution)/shard_map/ppermute | solution.py:41
  163.4 0.6 shard_map.97
  164.1 2.4 %collective-permute-start.29 = (f32[32,1536]{1,0:T(8,128)S(1)}, f32[32,1536]{1,0:T(8,128)S(1)}, u32[]{:S(2)}, u32[]{:S(2)}) collective-permute-start(f32[32,1536]{1,0:T(8,128)S(1)} %get-tuple-element.141), channel_id=1, source_target_pairs={{0,8},{1,9},{2,10},{3,11},{4,12},{5,13},{6,14},{7,15},{8,0},{9,1},... | collective-permute-start | bytes 589832 | tf_op jit(solution)/shard_map/ppermute | solution.py:41
  166.5 16.2 %collective-permute-done.21.refs_3_ = f32[64,1536]{1,0:T(8,128)S(1)} collective-permute-done((f32[64,1536]{1,0:T(8,128)S(1)}, f32[64,1536]{1,0:T(8,128)S(1)}, u32[]{:S(2)}, u32[]{:S(2)}) %collective-permute-start.21) | collective-permute-done | bytes 393248 | tf_op jit(solution)/shard_map/ppermute | solution.py:41
  184.0 2.9 %collective-permute-start.24 = (f32[16,1536]{1,0:T(8,128)S(1)}, f32[16,1536]{1,0:T(8,128)S(1)}, u32[]{:S(2)}, u32[]{:S(2)}) collective-permute-start(f32[16,1536]{1,0:T(8,128)S(1)} %get-tuple-element.135), channel_id=1, source_target_pairs={{0,16},{1,17},{2,18},{3,19},{4,20},{5,21},{6,22},{7,23},{8,24},{9,... | collective-permute-start | bytes 294920 | tf_op jit(solution)/shard_map/ppermute | solution.py:41
  187.0 0.8 collective-permute-start.25
  187.8 0.7 collective-permute-start.26
  188.5 1.0 pad_maximum_fusion
  190.1 1.9 collective-permute-start.31
  192.6 2.2 %collective-permute-start.30 = (f32[16,1536]{1,0:T(8,128)S(1)}, f32[16,1536]{1,0:T(8,128)S(1)}, u32[]{:S(2)}, u32[]{:S(2)}) collective-permute-start(f32[16,1536]{1,0:T(8,128)S(1)} %get-tuple-element.144), channel_id=1, source_target_pairs={{0,2},{1,3},{2,0},{3,1},{4,6},{5,7},{6,4},{7,5},{8,10},{9,11},{10,... | collective-permute-start | bytes 294920 | tf_op jit(solution)/shard_map/ppermute | solution.py:41
  194.8 1.0 collective-permute-done.26
  196.0 1.4 collective-permute-done.30
  198.1 0.8 copy.11
  (90 shorter events, 7.5 us)
Async XLA Ops:
  5.3 29.7 %collective-permute-start = (f32[256,512]{1,0:T(8,128)}, f32[256,512]{1,0:T(8,128)S(1)}, u32[]{:S(2)}, u32[]{:S(2)}) collective-permute-start(f32[256,512]{1,0:T(8,128)} %get-tuple-element.75.refs_1_), channel_id=1, source_target_pairs={{0,4},{1,5},{2,6},{3,7},{4,0},{5,1},{6,2},{7,3},{8,12},{9,13},{10,... | collective-permute-start | bytes 1572872 | tf_op jit(solution)/shard_map/ppermute | solution.py:36
  8.3 26.7 %collective-permute-start.1 = (f32[256,512]{1,0:T(8,128)}, f32[256,512]{1,0:T(8,128)}, u32[]{:S(2)}, u32[]{:S(2)}) collective-permute-start(f32[256,512]{1,0:T(8,128)} %get-tuple-element.75.refs_1_), channel_id=1, source_target_pairs={{4,8},{5,9},{6,10},{7,11},{8,4},{9,5},{10,6},{11,7},{12,16},{13,17... | collective-permute-start | bytes 1572872 | tf_op jit(solution)/shard_map/ppermute | solution.py:36
  9.8 8.9 %copy-start.1 = (f32[512,512]{1,0:T(8,128)S(1)}, f32[512,512]{1,0:T(8,128)}, u32[]{:S(2)}) copy-start(f32[512,512]{1,0:T(8,128)} %refs_1_.8) | copy-start | bytes 3145732
  9.8 8.9 %copy-start.6 = (s32[3]{0:T(128)S(1)}, s32[3]{0:T(128)}, u32[]{:S(2)}) copy-start(s32[3]{0:T(128)} %pad_add_fusion.scalars) | copy-start | bytes 40
  18.4 21.6 %slice-start = ((s8[9437184]{0:T(1024)(128)(4,1)}), s8[1048576]{0:T(1024)(128)(4,1)S(1)}, s32[]{:S(2)}) async-start(s8[9437184]{0:T(1024)(128)(4,1)} %bitcast.7), calls=%async_computation | async-start | bytes 2097152
  18.7 1.2 copy-start.2
  19.9 1.2 copy-start.5
  24.5 3.7 %copy-start = (f32[3,3,512,512]{3,2,1,0:T(8,128)S(1)}, f32[3,3,512,512]{3,2,1,0:T(8,128)}, u32[]{:S(2)}) copy-start(f32[3,3,512,512]{3,2,1,0:T(8,128)} %refs_2_.9) | copy-start | bytes 28311556
  28.2 1.0 copy-start.3
  28.2 1.2 copy-start.4
  28.2 1.4 copy-start.10
  28.2 11.8 %slice-start.1 = ((s8[9437184]{0:T(1024)(128)(4,1)}), s8[4194304]{0:T(1024)(128)(4,1)S(1)}, s32[]{:S(2)}) async-start(s8[9437184]{0:T(1024)(128)(4,1)} %bitcast.7), calls=%async_computation.1 | async-start | bytes 8388608
  28.2 11.8 %slice-start.2 = ((s8[9437184]{0:T(1024)(128)(4,1)}), s8[4194304]{0:T(1024)(128)(4,1)S(1)}, s32[]{:S(2)}) async-start(s8[9437184]{0:T(1024)(128)(4,1)} %bitcast.7), calls=%async_computation.2 | async-start | bytes 8388608
  28.9 6.0 %copy-start.13 = (f32[256,512]{1,0:T(8,128)S(1)}, f32[256,512]{1,0:T(8,128)}, u32[]{:S(2)}) copy-start(f32[256,512]{1,0:T(8,128)} %get-tuple-element.84.refs_5_) | copy-start | bytes 1572868
  29.0 6.0 %copy-start.14 = (f32[256,512]{1,0:T(8,128)S(1)}, f32[256,512]{1,0:T(8,128)}, u32[]{:S(2)}) copy-start(f32[256,512]{1,0:T(8,128)} %get-tuple-element.85.refs_6_) | copy-start | bytes 1572868
  30.7 36.6 %collective-permute-start.4 = (f32[256,512]{1,0:T(8,128)S(1)}, f32[256,512]{1,0:T(8,128)S(1)}, u32[]{:S(2)}, u32[]{:S(2)}) collective-permute-start(f32[256,512]{1,0:T(8,128)S(1)} %get-tuple-element.90.refs_1_.refs_2_), channel_id=1, source_target_pairs={{0,4},{1,5},{2,6},{3,7},{4,0},{5,1},{6,2},{7,3},{8,12},{9,13},{10,... | collective-permute-start | bytes 1572872 | tf_op jit(solution)/shard_map/ppermute | solution.py:36
  34.3 33.1 %collective-permute-start.5 = (f32[256,512]{1,0:T(8,128)S(1)}, f32[256,512]{1,0:T(8,128)S(1)}, u32[]{:S(2)}, u32[]{:S(2)}) collective-permute-start(f32[256,512]{1,0:T(8,128)S(1)} %get-tuple-element.90.refs_1_.refs_2_), channel_id=1, source_target_pairs={{4,8},{5,9},{6,10},{7,11},{8,4},{9,5},{10,6},{11,7},{12,16},{13,17... | collective-permute-start | bytes 1572872 | tf_op jit(solution)/shard_map/ppermute | solution.py:36
  37.7 37.3 %collective-permute-start.2 = (f32[256,512]{1,0:T(8,128)S(1)}, f32[256,512]{1,0:T(8,128)S(1)}, u32[]{:S(2)}, u32[]{:S(2)}) collective-permute-start(f32[256,512]{1,0:T(8,128)S(1)} %get-tuple-element.87.refs_1_), channel_id=1, source_target_pairs={{0,2},{1,3},{2,0},{3,1},{4,6},{5,7},{6,4},{7,5},{8,10},{9,11},{10,... | collective-permute-start | bytes 1572872 | tf_op jit(solution)/shard_map/ppermute | solution.py:36
  39.3 36.3 %collective-permute-start.3 = (f32[256,512]{1,0:T(8,128)S(1)}, f32[256,512]{1,0:T(8,128)S(1)}, u32[]{:S(2)}, u32[]{:S(2)}) collective-permute-start(f32[256,512]{1,0:T(8,128)S(1)} %get-tuple-element.87.refs_1_), channel_id=1, source_target_pairs={{2,4},{3,5},{4,2},{5,3},{6,8},{7,9},{8,6},{9,7},{10,12},{11,13},{1... | collective-permute-start | bytes 1572872 | tf_op jit(solution)/shard_map/ppermute | solution.py:36
  40.0 1.0 copy-start.9
  42.2 25.1 %copy-start.11 = (f32[256,512]{1,0:T(8,128)S(1)}, f32[256,512]{1,0:T(8,128)}, u32[]{:S(2)}) copy-start(f32[256,512]{1,0:T(8,128)} %get-tuple-element.96.refs_5_) | copy-start | bytes 1572868
  42.2 25.1 %copy-start.12 = (f32[256,512]{1,0:T(8,128)S(1)}, f32[256,512]{1,0:T(8,128)}, u32[]{:S(2)}) copy-start(f32[256,512]{1,0:T(8,128)} %get-tuple-element.97.refs_6_) | copy-start | bytes 1572868
  69.0 6.5 %copy-start.7 = (f32[256,512]{1,0:T(8,128)S(1)}, f32[256,512]{1,0:T(8,128)}, u32[]{:S(2)}) copy-start(f32[256,512]{1,0:T(8,128)} %get-tuple-element.93.refs_5_) | copy-start | bytes 1572868
  69.0 6.5 %copy-start.8 = (f32[256,512]{1,0:T(8,128)S(1)}, f32[256,512]{1,0:T(8,128)}, u32[]{:S(2)}) copy-start(f32[256,512]{1,0:T(8,128)} %get-tuple-element.94.refs_6_) | copy-start | bytes 1572868
  69.0 22.5 %collective-permute-start.10 = (f32[256,512]{1,0:T(8,128)S(1)}, f32[256,512]{1,0:T(8,128)S(1)}, u32[]{:S(2)}, u32[]{:S(2)}) collective-permute-start(f32[256,512]{1,0:T(8,128)S(1)} %get-tuple-element.104.refs_1_.refs_2_), channel_id=1, source_target_pairs={{0,2},{1,3},{2,0},{3,1},{4,6},{5,7},{6,4},{7,5},{8,10},{9,11},{10,... | collective-permute-start | bytes 1572872 | tf_op jit(solution)/shard_map/ppermute | solution.py:36
  70.6 21.6 %collective-permute-start.11 = (f32[256,512]{1,0:T(8,128)S(1)}, f32[256,512]{1,0:T(8,128)S(1)}, u32[]{:S(2)}, u32[]{:S(2)}) collective-permute-start(f32[256,512]{1,0:T(8,128)S(1)} %get-tuple-element.104.refs_1_.refs_2_), channel_id=1, source_target_pairs={{2,4},{3,5},{4,2},{5,3},{6,8},{7,9},{8,6},{9,7},{10,12},{11,13},{1... | collective-permute-start | bytes 1572872 | tf_op jit(solution)/shard_map/ppermute | solution.py:36
  75.0 19.0 %collective-permute-start.9 = (f32[256,1024]{1,0:T(8,128)S(1)}, f32[256,1024]{1,0:T(8,128)S(1)}, u32[]{:S(2)}, u32[]{:S(2)}) collective-permute-start(f32[256,1024]{1,0:T(8,128)S(1)} %get-tuple-element.108), channel_id=1, source_target_pairs={{0,1},{1,0},{2,3},{3,2},{4,5},{5,4},{6,7},{7,6},{8,9},{9,8},{10,11... | collective-permute-start | bytes 3145736 | tf_op jit(solution)/shard_map/ppermute | solution.py:41
  75.0 18.9 %collective-permute-start.8 = (f32[256,512]{1,0:T(8,128)S(1)}, f32[256,512]{1,0:T(8,128)S(1)}, u32[]{:S(2)}, u32[]{:S(2)}) collective-permute-start(f32[256,512]{1,0:T(8,128)S(1)} %get-tuple-element.107), channel_id=1, source_target_pairs={{0,1},{1,0},{2,3},{3,2},{4,5},{5,4},{6,7},{7,6},{8,9},{9,8},{10,11... | collective-permute-start | bytes 1572872 | tf_op jit(solution)/shard_map/ppermute | solution.py:41
  79.1 13.1 %copy-start.15 = (f32[256,512]{1,0:T(8,128)S(1)}, f32[256,512]{1,0:T(8,128)}, u32[]{:S(2)}) copy-start(f32[256,512]{1,0:T(8,128)} %get-tuple-element.109.refs_5_) | copy-start | bytes 1572868
  79.1 13.1 %copy-start.16 = (f32[256,512]{1,0:T(8,128)S(1)}, f32[256,512]{1,0:T(8,128)}, u32[]{:S(2)}) copy-start(f32[256,512]{1,0:T(8,128)} %get-tuple-element.110.refs_6_) | copy-start | bytes 1572868
  79.2 15.5 %collective-permute-start.6 = (f32[256,512]{1,0:T(8,128)S(1)}, f32[256,512]{1,0:T(8,128)S(1)}, u32[]{:S(2)}, u32[]{:S(2)}) collective-permute-start(f32[256,512]{1,0:T(8,128)S(1)} %get-tuple-element.102.refs_1_), channel_id=1, source_target_pairs={{0,1},{1,0},{2,3},{3,2},{4,5},{5,4},{6,7},{7,6},{8,9},{9,8},{10,11... | collective-permute-start | bytes 1572872 | tf_op jit(solution)/shard_map/ppermute | solution.py:36
  91.6 3.1 %collective-permute-start.7 = (f32[256,512]{1,0:T(8,128)S(1)}, f32[256,512]{1,0:T(8,128)S(1)}, u32[]{:S(2)}, u32[]{:S(2)}) collective-permute-start(f32[256,512]{1,0:T(8,128)S(1)} %get-tuple-element.102.refs_1_), channel_id=1, source_target_pairs={{1,2},{2,1},{3,4},{4,3},{5,6},{6,5},{7,8},{8,7},{9,10},{10,9},{11,... | collective-permute-start | bytes 1572872 | tf_op jit(solution)/shard_map/ppermute | solution.py:36
  98.8 34.4 %collective-permute-start.18 = (f32[256,1024]{1,0:T(8,128)S(1)}, f32[256,1024]{1,0:T(8,128)S(1)}, u32[]{:S(2)}, u32[]{:S(2)}) collective-permute-start(f32[256,1024]{1,0:T(8,128)S(1)} %get-tuple-element.123), channel_id=1, source_target_pairs={{0,1},{1,0},{2,3},{3,2},{4,5},{5,4},{6,7},{7,6},{8,9},{9,8},{10,11... | collective-permute-start | bytes 3145736 | tf_op jit(solution)/shard_map/ppermute | solution.py:41
  111.9 9.1 %collective-permute-start.12 = (f32[256,512]{1,0:T(8,128)S(1)}, f32[256,512]{1,0:T(8,128)S(1)}, u32[]{:S(2)}, u32[]{:S(2)}) collective-permute-start(f32[256,512]{1,0:T(8,128)S(1)} %get-tuple-element.115.refs_2_.refs_1_), channel_id=1, source_target_pairs={{0,1},{1,0},{2,3},{3,2},{4,5},{5,4},{6,7},{7,6},{8,9},{9,8},{10,11... | collective-permute-start | bytes 1572872 | tf_op jit(solution)/shard_map/ppermute | solution.py:36
  112.0 9.0 %collective-permute-start.13 = (f32[256,512]{1,0:T(8,128)S(1)}, f32[256,512]{1,0:T(8,128)S(1)}, u32[]{:S(2)}, u32[]{:S(2)}) collective-permute-start(f32[256,512]{1,0:T(8,128)S(1)} %get-tuple-element.115.refs_2_.refs_1_), channel_id=1, source_target_pairs={{1,2},{2,1},{3,4},{4,3},{5,6},{6,5},{7,8},{8,7},{9,10},{10,9},{11,... | collective-permute-start | bytes 1572872 | tf_op jit(solution)/shard_map/ppermute | solution.py:36
  112.9 20.2 %collective-permute-start.17 = (f32[256,512]{1,0:T(8,128)S(1)}, f32[256,512]{1,0:T(8,128)S(1)}, u32[]{:S(2)}, u32[]{:S(2)}) collective-permute-start(f32[256,512]{1,0:T(8,128)S(1)} %get-tuple-element.122), channel_id=1, source_target_pairs={{0,1},{1,0},{2,3},{3,2},{4,5},{5,4},{6,7},{7,6},{8,9},{9,8},{10,11... | collective-permute-start | bytes 1572872 | tf_op jit(solution)/shard_map/ppermute | solution.py:41
  117.1 23.0 %collective-permute-start.16 = (f32[128,1536]{1,0:T(8,128)S(1)}, f32[128,1536]{1,0:T(8,128)S(1)}, u32[]{:S(2)}, u32[]{:S(2)}) collective-permute-start(f32[128,1536]{1,0:T(8,128)S(1)} %get-tuple-element.121), channel_id=1, source_target_pairs={{0,4},{1,5},{2,6},{3,7},{4,0},{5,1},{6,2},{7,3},{8,12},{9,13},{10,... | collective-permute-start | bytes 2359304 | tf_op jit(solution)/shard_map/ppermute | solution.py:41
  125.1 20.4 %collective-permute-start.15 = (f32[256,1024]{1,0:T(8,128)S(1)}, f32[256,1024]{1,0:T(8,128)S(1)}, u32[]{:S(2)}, u32[]{:S(2)}) collective-permute-start(f32[256,1024]{1,0:T(8,128)S(1)} %get-tuple-element.120), channel_id=1, source_target_pairs={{0,1},{1,0},{2,3},{3,2},{4,5},{5,4},{6,7},{7,6},{8,9},{9,8},{10,11... | collective-permute-start | bytes 3145736 | tf_op jit(solution)/shard_map/ppermute | solution.py:41
  133.9 29.5 %collective-permute-start.22 = (f32[128,1536]{1,0:T(8,128)S(1)}, f32[128,1536]{1,0:T(8,128)S(1)}, u32[]{:S(2)}, u32[]{:S(2)}) collective-permute-start(f32[128,1536]{1,0:T(8,128)S(1)} %get-tuple-element.130), channel_id=1, source_target_pairs={{0,4},{1,5},{2,6},{3,7},{4,0},{5,1},{6,2},{7,3},{8,12},{9,13},{10,... | collective-permute-start | bytes 2359304 | tf_op jit(solution)/shard_map/ppermute | solution.py:41
  134.7 10.8 %collective-permute-start.14 = (f32[256,512]{1,0:T(8,128)S(1)}, f32[256,512]{1,0:T(8,128)S(1)}, u32[]{:S(2)}, u32[]{:S(2)}) collective-permute-start(f32[256,512]{1,0:T(8,128)S(1)} %get-tuple-element.119), channel_id=1, source_target_pairs={{0,1},{1,0},{2,3},{3,2},{4,5},{5,4},{6,7},{7,6},{8,9},{9,8},{10,11... | collective-permute-start | bytes 1572872 | tf_op jit(solution)/shard_map/ppermute | solution.py:41
  140.8 22.0 %collective-permute-start.23 = (f32[64,1536]{1,0:T(8,128)S(1)}, f32[64,1536]{1,0:T(8,128)S(1)}, u32[]{:S(2)}, u32[]{:S(2)}) collective-permute-start(f32[64,1536]{1,0:T(8,128)S(1)} %get-tuple-element.131), channel_id=1, source_target_pairs={{0,16},{1,17},{2,18},{3,19},{4,20},{5,21},{6,22},{7,23},{8,24},{9,... | collective-permute-start | bytes 1179656 | tf_op jit(solution)/shard_map/ppermute | solution.py:41
  146.2 20.3 %collective-permute-start.19 = (f32[64,1536]{1,0:T(8,128)S(1)}, f32[64,1536]{1,0:T(8,128)S(1)}, u32[]{:S(2)}, u32[]{:S(2)}) collective-permute-start(f32[64,1536]{1,0:T(8,128)S(1)} %get-tuple-element.127), channel_id=1, source_target_pairs={{0,8},{1,9},{2,10},{3,11},{4,12},{5,13},{6,14},{7,15},{8,0},{9,1},... | collective-permute-start | bytes 1179656 | tf_op jit(solution)/shard_map/ppermute | solution.py:41
  146.3 20.2 %collective-permute-start.20 = (f32[64,1536]{1,0:T(8,128)S(1)}, f32[64,1536]{1,0:T(8,128)S(1)}, u32[]{:S(2)}, u32[]{:S(2)}) collective-permute-start(f32[64,1536]{1,0:T(8,128)S(1)} %get-tuple-element.128), channel_id=1, source_target_pairs={{0,2},{1,3},{2,0},{3,1},{4,6},{5,7},{6,4},{7,5},{8,10},{9,11},{10,... | collective-permute-start | bytes 1179656 | tf_op jit(solution)/shard_map/ppermute | solution.py:41
  148.5 34.1 %collective-permute-start.21 = (f32[64,1536]{1,0:T(8,128)S(1)}, f32[64,1536]{1,0:T(8,128)S(1)}, u32[]{:S(2)}, u32[]{:S(2)}) collective-permute-start(f32[64,1536]{1,0:T(8,128)S(1)} %get-tuple-element.129), channel_id=1, source_target_pairs={{0,10},{1,11},{2,8},{3,9},{4,14},{5,15},{6,12},{7,13},{8,2},{9,3},... | collective-permute-start | bytes 1179656 | tf_op jit(solution)/shard_map/ppermute | solution.py:41
  164.0 19.4 %collective-permute-start.27 = (f32[64,1536]{1,0:T(8,128)S(1)}, f32[64,1536]{1,0:T(8,128)S(1)}, u32[]{:S(2)}, u32[]{:S(2)}) collective-permute-start(f32[64,1536]{1,0:T(8,128)S(1)} %get-tuple-element.138), channel_id=1, source_target_pairs={{0,16},{1,17},{2,18},{3,19},{4,20},{5,21},{6,22},{7,23},{8,24},{9,... | collective-permute-start | bytes 1179656 | tf_op jit(solution)/shard_map/ppermute | solution.py:41
  164.1 25.5 %collective-permute-start.29 = (f32[32,1536]{1,0:T(8,128)S(1)}, f32[32,1536]{1,0:T(8,128)S(1)}, u32[]{:S(2)}, u32[]{:S(2)}) collective-permute-start(f32[32,1536]{1,0:T(8,128)S(1)} %get-tuple-element.141), channel_id=1, source_target_pairs={{0,8},{1,9},{2,10},{3,11},{4,12},{5,13},{6,14},{7,15},{8,0},{9,1},... | collective-permute-start | bytes 589832 | tf_op jit(solution)/shard_map/ppermute | solution.py:41
  184.0 8.1 %collective-permute-start.28 = (f32[32,1536]{1,0:T(8,128)S(1)}, f32[32,1536]{1,0:T(8,128)S(1)}, u32[]{:S(2)}, u32[]{:S(2)}) collective-permute-start(f32[32,1536]{1,0:T(8,128)S(1)} %get-tuple-element.140), channel_id=1, source_target_pairs={{0,8},{1,9},{2,10},{3,11},{4,12},{5,13},{6,14},{7,15},{8,0},{9,1},... | collective-permute-start | bytes 589832 | tf_op jit(solution)/shard_map/ppermute | solution.py:41
  184.0 10.8 %collective-permute-start.24 = (f32[16,1536]{1,0:T(8,128)S(1)}, f32[16,1536]{1,0:T(8,128)S(1)}, u32[]{:S(2)}, u32[]{:S(2)}) collective-permute-start(f32[16,1536]{1,0:T(8,128)S(1)} %get-tuple-element.135), channel_id=1, source_target_pairs={{0,16},{1,17},{2,18},{3,19},{4,20},{5,21},{6,22},{7,23},{8,24},{9,... | collective-permute-start | bytes 294920 | tf_op jit(solution)/shard_map/ppermute | solution.py:41
  187.0 7.8 %collective-permute-start.25 = (f32[16,1536]{1,0:T(8,128)S(1)}, f32[16,1536]{1,0:T(8,128)S(1)}, u32[]{:S(2)}, u32[]{:S(2)}) collective-permute-start(f32[16,1536]{1,0:T(8,128)S(1)} %get-tuple-element.136), channel_id=1, source_target_pairs={{0,4},{1,5},{2,6},{3,7},{4,0},{5,1},{6,2},{7,3},{8,12},{9,13},{10,... | collective-permute-start | bytes 294920 | tf_op jit(solution)/shard_map/ppermute | solution.py:41
  187.8 8.0 %collective-permute-start.26 = (f32[16,1536]{1,0:T(8,128)S(1)}, f32[16,1536]{1,0:T(8,128)S(1)}, u32[]{:S(2)}, u32[]{:S(2)}) collective-permute-start(f32[16,1536]{1,0:T(8,128)S(1)} %get-tuple-element.137), channel_id=1, source_target_pairs={{0,20},{1,21},{2,22},{3,23},{4,16},{5,17},{6,18},{7,19},{8,28},{9,... | collective-permute-start | bytes 294920 | tf_op jit(solution)/shard_map/ppermute | solution.py:41
  190.1 5.8 %collective-permute-start.31 = (f32[16,1536]{1,0:T(8,128)S(1)}, f32[16,1536]{1,0:T(8,128)S(1)}, u32[]{:S(2)}, u32[]{:S(2)}) collective-permute-start(f32[16,1536]{1,0:T(8,128)S(1)} %get-tuple-element.145), channel_id=1, source_target_pairs={{0,2},{1,3},{2,0},{3,1},{4,6},{5,7},{6,4},{7,5},{8,10},{9,11},{10,... | collective-permute-start | bytes 294920 | tf_op jit(solution)/shard_map/ppermute | solution.py:41
  192.6 4.8 %collective-permute-start.30 = (f32[16,1536]{1,0:T(8,128)S(1)}, f32[16,1536]{1,0:T(8,128)S(1)}, u32[]{:S(2)}, u32[]{:S(2)}) collective-permute-start(f32[16,1536]{1,0:T(8,128)S(1)} %get-tuple-element.144), channel_id=1, source_target_pairs={{0,2},{1,3},{2,0},{3,1},{4,6},{5,7},{6,4},{7,5},{8,10},{9,11},{10,... | collective-permute-start | bytes 294920 | tf_op jit(solution)/shard_map/ppermute | solution.py:41

commit v2 on v1

--- a/solution.py
+++ b/solution.py
@@ -13,17 +13,10 @@
 F32 = jnp.float32
 STRIP = 32
 PIECES = (2,)
-GROUPS = (((0,), (1, 3), (2, 4)), ((0,), (2,), (4,), (3,), (1,)), ((0,), (2,), (4,), (3,), (1,)))
-FIRST_SIXTEENTHS = 8
+GROUPS = (((0,), (1, 2), (3, 4)), ((0,), (2,), (1, 3), (4,)), ((0,), (3,), (2, 4), (1,)))
+FIRST_SIXTEENTHS = 7
 UNIT = 5 * 10**9
-ORDER = (
-    ("top", 0), ("prep", 0), ("turn", 0), ("w2", 0), ("ca2", 0), ("aa2", 0),
-    ("w1", 0), ("cb2", 0), ("ca1", 0), ("m2", 0), ("ab2", 0), ("t2", 0), ("aa1", 0),
-    ("w0", 0), ("cb1", 0), ("ca0", 0), ("m1", 0), ("ab1", 4), ("r2", 0), ("aa0", 0),
-    ("t1", 0), ("m0", 0), ("cb0", 0),
-    ("ab0", 0), ("t0", 0), ("r1", 0), ("r2", 0), ("r0", 0), ("r2", 0), ("r1", 0),
-    ("r0", 0), ("r1", 0), ("r2", 0), ("r1", 0),
-)
+ORDER = (('top', 0), ('prep', 0), ('w', 6), ('ca2', 1), ('cb2', 6), ('turn', 2), ('aa2', 1), ('ca1', 4), ('ab2', 0), ('t2', 1), ('m2', 2), ('aa1', 3), ('ca0', 0), ('cb1', 0), ('r2', 0), ('ab1', 1), ('t1', 10), ('cb0', 1), ('r1', 3), ('t0', 6), ('ab0', 0), ('r2', 4), ('r1', 0), ('r0', 0), ('r0', 0), ('r2', 0), ('r1', 6), ('aa0', 1))
 
 
 def paired(array, jump, parity):
@@ -148,10 +141,10 @@
         known = [g for g in (tuple(b for b in bits if b < width) for bits in layer) if g]
         listed = [b for g in known for b in g]
         groups.append(known + [(b,) for b in range(width) if b not in listed])
-    parity = jnp.stack([(me // jump) % 2 for jump in jumps]).astype(jnp.int32)
+    scalars = jnp.stack([*((me // jump) % 2 for jump in jumps), me]).astype(jnp.int32)
     cut = FIRST_SIXTEENTHS * bins // 16
     spans = ((0, cut), (cut, bins))
-    line = Line(parity)
+    line = Line(scalars)
     full = (bins, channels)
     square = (channels, channels)
     parts = [(stop - start, channels) for start, stop in spans]
@@ -222,38 +215,35 @@
         ins = [features, preacts, teacher, cotangent]
         return line(body, ins, [full] * 2 + [parts[0]] * 4 + [parts[1]] * 6, 56)
 
-    def weights(layer):
-        def body(_, *refs):
-            for source, target in zip(refs[:3], refs[3:]):
-                target[...] = source[...]
-
-        block = (pl.Squeezed(), pl.Squeezed(), channels, channels)
-        ins = [
-            (kernels, pl.BlockSpec(block, lambda i, s: (layer, 2 * s[layer], 0, 0))),
-            (kernels, pl.BlockSpec(block, lambda i, s: (layer, 1, 0, 0))),
-            (kernels, pl.BlockSpec(block, lambda i, s: (layer, 2 - 2 * s[layer], 0, 0))),
-        ]
-        return line(body, ins, [square] * 3)
+    def weights():
+        def body(scalars, k_ref, *targets):
+            for layer in range(LAYERS):
+                side = 2 * scalars[layer]
+                for n, k in enumerate((side, 1, 2 - side)):
+                    targets[3 * layer + n][...] = k_ref[layer, k]
+
+        out = line(body, [kernels], [square] * (3 * LAYERS), 32)
+        return [out[3 * layer : 3 * layer + 3] for layer in range(LAYERS)]
 
     def turn(xs):
         block = channels // devices
-        sources = []
-        for layer in range(LAYERS):
-            row = jnp.arange(channels, dtype=jnp.int32)
+        uses = [(0, 0), (0, 1), (1, 1), (1, 2), (2, 2)]
+
+        def body(scalars, *refs):
+            row = lax.broadcasted_iota(jnp.int32, (channels, 1), 0)
             index = row // block
-            target = jnp.zeros_like(row)
-            for place, bit in enumerate(b for g in groups[layer] for b in g):
-                target = target | (((index >> (width - 1 - place)) & 1) << bit)
-            sources.append((target ^ me) * block + row % block)
-        sources = jnp.stack(sources)[:, :, None]
-
-        def body(_, source_ref, *refs):
             lanes = lax.broadcasted_iota(jnp.int32, (channels, channels), 1)
-            for l in range(LAYERS):
-                pick = jnp.where(lanes == source_ref[l], 1.0, 0.0)
-                refs[LAYERS + l][...] = dot_nt(pick, refs[l][...])
-
-        return line(body, [sources, *xs], [(channels, bins)] * LAYERS)
+            picks = []
+            for layer in range(LAYERS):
+                target = jnp.zeros_like(row)
+                for place, bit in enumerate(b for g in groups[layer] for b in g):
+                    target = target | (((index >> (width - 1 - place)) & 1) << bit)
+                source = (target ^ scalars[LAYERS]) * block + row % block
+                picks.append(jnp.where(lanes == source, 1.0, 0.0))
+            for n, (x, order) in enumerate(uses):
+                refs[LAYERS + n][...] = dot_nt(picks[order], refs[x][...])
+
+        return dict(zip(uses, line(body, xs, [(channels, bins)] * len(uses))))
 
     def center(g, gu, w, carried=None):
         carry = [] if carried is None else [carried]
@@ -284,31 +274,44 @@
 
     rows = channels // 2
 
-    def middle(layer, x, gu_a, gu_b, work):
+    def add(layer, x, body, inputs, taps, work):
+        keep, send = line(body, [x, *inputs], [(rows, len(taps) * channels)] * 2, work=work)
+        sums[layer].add(send, keep)
+        columns[layer].extend(taps)
+
+    def store(outs, place, value):
+        for n, out_ref in enumerate(outs):
+            out_ref[:, place] = value[rows * n : rows * (n + 1), :]
+
+    def middle(layer, work):
         def body(_, x_ref, a_ref, b_ref, *outs):
             both = jnp.concatenate([a_ref[...], b_ref[...]], axis=0)
-            value = dot(x_ref[...], both)
-            for n, out_ref in enumerate(outs):
-                out_ref[...] = value[rows * n : rows * (n + 1), :]
-
-        keep, send = line(body, [x, gu_a, gu_b], [(rows, channels)] * 2, work=work)
-        sums[layer].add(send, keep)
-
-    def terms(layer, x, sides_a, sides_b, work):
+            store(outs, slice(0, channels), dot(x_ref[...], both))
+
+        add(layer, xt[layer, layer], body, [gu["a", layer], gu["b", layer]], [(layer, 1)], work)
+
+    def terms(layer, work):
+        below = layer - 1
+        ins = [*halos["a", layer], *halos["b", layer]]
+        if layer:
+            ins += [gu["a", below], gu["b", below], xt[below, layer]]
+
         def body(s_ref, x_ref, *refs):
+            outs = refs[len(ins) :]
             for k in range(2):
                 column = s_ref[layer] if k == 0 else 1 - s_ref[layer]
                 place = pl.ds(pl.multiple_of(column * channels, channels), channels)
                 both = jnp.concatenate([refs[k][...], refs[2 + k][...]], axis=0)
-                value = dot(x_ref[...], both)
-                for n, out_ref in enumerate(refs[4:]):
-                    out_ref[:, place] = value[rows * n : rows * (n + 1), :]
-
-        shapes = [(rows, 2 * channels)] * 2
-        keep, send = line(body, [x, *sides_a, *sides_b], shapes, work=work)
-        sums[layer].add(send, keep)
+                store(outs, place, dot(x_ref[...], both))
+            if layer:
+                both = jnp.concatenate([refs[4][...], refs[5][...]], axis=0)
+                store(outs, slice(2 * channels, 3 * channels), dot(refs[6][...], both))
+
+        taps = [(layer, 0), (layer, 2)] + ([(below, 1)] if layer else [])
+        add(layer, xt[layer, layer], body, ins, taps, work)
 
     sums = [Scatter(line, groups[layer]) for layer in range(LAYERS)]
+    columns = [[] for _ in range(LAYERS)]
     w, base, g, gu, halos = {}, {}, {}, {}, {}
     pull, slope = {}, {}
     for name, work in ORDER:
@@ -318,13 +321,14 @@
             halos["a", 2] = halo(gu["a", 2], 2)
         elif name == "prep":
             x1, x2, *pairs, g["b"], carried = prepare()
+            gu["b", 2] = carried
             for c, key in enumerate("ab"):
                 h = pairs[4 * c : 4 * c + 4]
                 pull[key, 1], slope[key, 1], pull[key, 2], slope[key, 2] = h
         elif name == "turn":
             xt = turn((features, x1, x2))
-        elif kind == "w":
-            w[layer] = weights(layer)
+        elif name == "w":
+            w = weights()
         elif name == "ca2":
             base["a"], gu["b", 2] = center(g["a"], gu["a", 2], w[2][1], carried)
             halos["b", 2] = halo(gu["b", 2], 2)
@@ -342,18 +346,21 @@
             else:
                 (g[key],) = advance(*args, work=work)
         elif kind == "m":
-            middle(layer, xt[layer], gu["a", layer], gu["b", layer], work)
+            middle(layer, work)
         elif kind == "t":
-            terms(layer, xt[layer], halos["a", layer], halos["b", layer], work)
-        else:
+            terms(layer, work)
+        elif sums[layer].groups:
             sums[layer].step(work)
     for s in sums:
         while s.groups:
             s.step(0)
     done = [s.result() for s in sums]
-    grads = jnp.stack(done) * scale
-    grads = grads.reshape(LAYERS, channels // devices, 3, channels).transpose(0, 2, 1, 3)
-    grads = jnp.stack([grads[:, 1], grads[:, 0], grads[:, 2]], axis=1)
+    taps = {}
+    for total, names in zip(done, columns):
+        for n, tap in enumerate(names):
+            taps[tap] = total[:, n * channels : (n + 1) * channels]
+    grads = jnp.stack([jnp.stack([taps[layer, k] for k in range(3)]) for layer in range(LAYERS)])
+    grads = grads * scale
     return jnp.concatenate([g["a"], g["b"]], axis=0), grads
 
 

time: 199 us -> 179 us (0.90)
  waiting for transfers between devices: 68.6 us -> 53.7 us
  Pallas kernels: 55.5 us -> 52.4 us
  local copies, waits for them, and re-layouts: 8.55 us -> 5.75 us
    ppermute x20, waiting for transfers between devices: 36.8 us -> 20.2 us  [swapped(): return lax.ppermute(array, 'seq', [(i, i ^ mask) for i in range(devices)])]
    ppermute x12, starting transfers between devices: 15.1 us -> 21.2 us  [paired(): return lax.ppermute(array, 'seq', pairs)]
    ppermute x20, starting transfers between devices: 47.6 us -> 42 us  [swapped(): return lax.ppermute(array, 'seq', [(i, i ^ mask) for i in range(devices)])]
    pallas_call x34 -> x28, Pallas kernels: 55.5 us -> 52.4 us  [__call__(): pl.pallas_call(kernel, grid_spec=pltpu.PrefetchScalarGridSpec(num_scalar_...]
    unnamed x41 -> x40, local copies, waits for them, and re-layouts: 7.83 us -> 5.72 us
where the time goes in v2:
time: 179 us
  starting transfers between devices  63.2 us (35%)
  waiting for transfers between devices  53.7 us (30%)
  Pallas kernels  52.4 us (29%)
  local copies, waits for them, and re-layouts  5.75 us (3%)
  other arithmetic  2.52 us (1%)
    pallas_call x28, Pallas kernels, __call__(): pl.pallas_call(kernel, grid_spec=pltpu.PrefetchScalarGridSpec(num_scalar_...  52.4 us
    ppermute x20, starting transfers between devices, swapped(): return lax.ppermute(array, 'seq', [(i, i ^ mask) for i in range(devices)])  42 us
    ppermute x12, waiting for transfers between devices, paired(): return lax.ppermute(array, 'seq', pairs)  33.5 us
    ppermute x12, starting transfers between devices, paired(): return lax.ppermute(array, 'seq', pairs)  21.2 us
    ppermute x20, waiting for transfers between devices, swapped(): return lax.ppermute(array, 'seq', [(i, i ^ mask) for i in range(devices)])  20.2 us
    unnamed x40, local copies, waits for them, and re-layouts  5.72 us
  transfers between devices with their start and end apart: 32, of which 8 were waited for; matrix products, arithmetic and copies ran while one was open for 1% of the time, Pallas kernels for 24%

profile of v2, /device:TPU:0, one launch (start us, length us, event | category | flops | bytes accessed | tf_op | source)
XLA Modules:
  0.0 179.0 jit_solution(8823129646225533665)
XLA Ops:
  0.7 0.7 pad_add_fusion.scalars
  1.4 3.8 %shard_map.68 = (f32[224,512]{1,0:T(8,128)}, f32[224,512]{1,0:T(8,128)}) custom-call(s32[4]{0:T(128)} %pad_add_fusion.scalars, f32[512,512]{1,0:T(8,128)} %refs_0_.7, f32[3,512,512]{2,1,0:T(8,128)} %refs_1_.3, f32[3,512,512]{2,1,0:T(8,128)} %refs_1_.3, f32[3,512,512]{2,1,0:T(8,128)} %refs_1_.3, f32[3,512,512]{2,1,0:T(8,128)} %refs_2_.3, f32[512,512]{1,0:T(8,128)} %refs_3_.3), custom_call_target="tpu_custom_call" | custom-call | bytes 1024 | tf_op jit(solution)/shard_map/pallas_call | solution.py:73
  5.2 3.0 %collective-permute-start = (f32[224,512]{1,0:T(8,128)}, f32[224,512]{1,0:T(8,128)S(1)}, u32[]{:S(2)}, u32[]{:S(2)}) collective-permute-start(f32[224,512]{1,0:T(8,128)} %get-tuple-element.73.refs_1_), channel_id=1, source_target_pairs={{0,4},{1,5},{2,6},{3,7},{4,0},{5,1},{6,2},{7,3},{8,12},{9,13},{10,... | collective-permute-start | bytes 1376264 | tf_op jit(solution)/shard_map/ppermute | solution.py:29
  8.1 0.7 collective-permute-start.1
  8.8 8.6 %shard_map.69 = (f32[512,512]{1,0:T(8,128)}, f32[512,512]{1,0:T(8,128)}, f32[224,512]{1,0:T(8,128)}, f32[224,512]{1,0:T(8,128)}, f32[224,512]{1,0:T(8,128)}, /*i...) custom-call(s32[4]{0:T(128)} %pad_add_fusion.scalars, ...), custom_call_target="tpu_custom_call" | custom-call | bytes 1024 | tf_op jit(solution)/shard_map/pallas_call | solution.py:73
  17.4 3.7 %copy-done.1 = f32[3,3,512,512]{3,2,1,0:T(8,128)S(1)} copy-done((f32[3,3,512,512]{3,2,1,0:T(8,128)S(1)}, f32[3,3,512,512]{3,2,1,0:T(8,128)}, u32[]{:S(2)}) %copy-start.1) | copy-done | bytes 9437208
  21.1 1.2 copy-done.2
  22.3 1.1 shard_map.70
  23.6 1.2 shard_map.71
  24.9 4.3 %collective-permute-start.4 = (f32[288,512]{1,0:T(8,128)S(1)}, f32[288,512]{1,0:T(8,128)S(1)}, u32[]{:S(2)}, u32[]{:S(2)}) collective-permute-start(f32[288,512]{1,0:T(8,128)S(1)} %get-tuple-element.85.refs_1_.refs_2_), channel_id=1, source_target_pairs={{0,4},{1,5},{2,6},{3,7},{4,0},{5,1},{6,2},{7,3},{8,12},{9,13},{10,... | collective-permute-start | bytes 1769480 | tf_op jit(solution)/shard_map/ppermute | solution.py:29
  29.2 0.7 collective-permute-start.5
  29.9 1.2 shard_map.72.refs_3_.refs_0_
  31.8 5.4 %shard_map.73 = (f32[512,512]{1,0:T(8,128)S(1)}, f32[512,512]{1,0:T(8,128)S(1)}, f32[512,512]{1,0:T(8,128)S(1)}, f32[512,512]{1,0:T(8,128)S(1)}, f32[512,512]{1,0:T(8,128)S(1)}) custom-call(s32[4]{0:T(128)S(1)} %copy-done.13, f32[512,512]{1,0:T(8,128)S(1)} %copy-done, f32[512,512]{1,0:T(8,128)S(1)} %copy-done.3, f32[512,512]{1,0:T(8,128)S(1)} %copy-done.7, ...), custom_call_target="tpu_custom_call" | custom-call | bytes 1024 | tf_op jit(solution)/shard_map/pallas_call | solution.py:73
  37.2 1.7 shard_map.74
  39.0 1.6 collective-permute-start.2
  40.5 0.7 collective-permute-start.3
  41.2 1.2 shard_map.75.refs_7_.refs_0_
  42.4 21.3 %collective-permute-done.4.refs_1_.refs_3_ = f32[288,512]{1,0:T(8,128)S(1)} collective-permute-done((f32[288,512]{1,0:T(8,128)S(1)}, f32[288,512]{1,0:T(8,128)S(1)}, u32[]{:S(2)}, u32[]{:S(2)}) %collective-permute-start.4) | collective-permute-done | bytes 589856 | tf_op jit(solution)/shard_map/ppermute | solution.py:29
  63.7 1.7 shard_map.76
  65.5 1.6 collective-permute-start.8
  67.0 0.9 collective-permute-start.9
  67.9 3.3 %shard_map.77 = (f32[256,1536]{1,0:T(8,128)S(1)}, f32[256,1536]{1,0:T(8,128)S(1)}) custom-call(s32[4]{0:T(128)S(1)} %copy-done.13, f32[512,512]{1,0:T(8,128)S(1)} %get-tuple-element.94.refs_0_, f32[224,512]{1,0:T(8,128)S(1)} %collective-permute-done.refs_1_, f32[224,512]{1,0:T(8,128)S(1)} %collective-permute-done.1.refs_2_, ...), custom_call_target="tpu_custom_call" | custom-call | flops 5000000000 | bytes 1024 | tf_op jit(solution)/shard_map/pallas_call | solution.py:73
  71.3 1.6 shard_map.78
  72.9 0.5 collective-permute-start.11
  73.4 1.8 shard_map.79
  75.2 1.2 shard_map.80.refs_3_.refs_0_
  76.5 1.2 shard_map.81.refs_4_.refs_0_
  77.7 0.8 shard_map.82
  78.5 12.3 %collective-permute-done.8.refs_1_.refs_3_ = f32[288,512]{1,0:T(8,128)S(1)} collective-permute-done((f32[288,512]{1,0:T(8,128)S(1)}, f32[288,512]{1,0:T(8,128)S(1)}, u32[]{:S(2)}, u32[]{:S(2)}) %collective-permute-start.8) | collective-permute-done | bytes 589856 | tf_op jit(solution)/shard_map/ppermute | solution.py:29
  90.8 1.7 shard_map.83
  92.5 3.3 %shard_map.84 = (f32[256,1536]{1,0:T(8,128)S(1)}, f32[256,1536]{1,0:T(8,128)S(1)}) custom-call(s32[4]{0:T(128)S(1)} %copy-done.13, f32[512,512]{1,0:T(8,128)S(1)} %get-tuple-element.106.refs_0_, f32[224,512]{1,0:T(8,128)S(1)} %collective-permute-done.2.refs_1_, f32[224,512]{1,0:T(8,128)S(1)} %collective-permute-done.3.refs_2_, ...), custom_call_target="tpu_custom_call" | custom-call | flops 49999998976 | bytes 1024 | tf_op jit(solution)/shard_map/pallas_call | solution.py:73
  95.9 0.5 collective-permute-start.6
  96.4 0.7 collective-permute-start.7
  97.1 5.8 %collective-permute-start.15 = (f32[288,512]{1,0:T(8,128)S(1)}, f32[288,512]{1,0:T(8,128)S(1)}, u32[]{:S(2)}, u32[]{:S(2)}) collective-permute-start(f32[288,512]{1,0:T(8,128)S(1)} %get-tuple-element.112.refs_6_.refs_1_), channel_id=1, source_target_pairs={{0,1},{1,0},{2,3},{3,2},{4,5},{5,4},{6,7},{7,6},{8,9},{9,8},{10,11... | collective-permute-start | bytes 1769480 | tf_op jit(solution)/shard_map/ppermute | solution.py:29
  102.9 0.9 collective-permute-start.16
  103.8 1.2 shard_map.85.refs_2_.refs_0_
  105.1 2.9 %collective-permute-start.14 = (f32[128,2048]{1,0:T(8,128)S(1)}, f32[128,2048]{1,0:T(8,128)S(1)}, u32[]{:S(2)}, u32[]{:S(2)}) collective-permute-start(f32[128,2048]{1,0:T(8,128)S(1)} %get-tuple-element.119), channel_id=1, source_target_pairs={{0,8},{1,9},{2,10},{3,11},{4,12},{5,13},{6,14},{7,15},{8,0},{9,1},... | collective-permute-start | bytes 3145736 | tf_op jit(solution)/shard_map/ppermute | solution.py:34
  107.9 0.7 shard_map.86
  108.6 1.7 collective-permute-start.13
  110.3 2.4 %shard_map.87 = (f32[256,1024]{1,0:T(8,128)S(1)}, f32[256,1024]{1,0:T(8,128)S(1)}) custom-call(s32[4]{0:T(128)S(1)} %copy-done.13, f32[512,512]{1,0:T(8,128)S(1)} %get-tuple-element.86.refs_7_.refs_0_, f32[224,512]{1,0:T(8,128)S(1)} %collective-permute-done.6.refs_1_, f32[224,512]{1,0:T(8,128)S(1)} %collective-permute-done.7.refs_2_, ...), custom_call_target="tpu_custom_call" | custom-call | flops 30000001024 | bytes 1024 | tf_op jit(solution)/shard_map/pallas_call | solution.py:73
  112.8 16.0 %collective-permute-start.23 = (f32[256,1024]{1,0:T(8,128)S(1)}, f32[256,1024]{1,0:T(8,128)S(1)}, u32[]{:S(2)}, u32[]{:S(2)}) collective-permute-start(f32[256,1024]{1,0:T(8,128)S(1)} %get-tuple-element.129), channel_id=1, source_target_pairs={{0,1},{1,0},{2,3},{3,2},{4,5},{5,4},{6,7},{7,6},{8,9},{9,8},{10,11... | collective-permute-start | bytes 3145736 | tf_op jit(solution)/shard_map/ppermute | solution.py:34
  128.7 1.7 shard_map.88.refs_2_
  130.5 7.4 %collective-permute-done.14.refs_1_ = f32[128,2048]{1,0:T(8,128)S(1)} collective-permute-done((f32[128,2048]{1,0:T(8,128)S(1)}, f32[128,2048]{1,0:T(8,128)S(1)}, u32[]{:S(2)}, u32[]{:S(2)}) %collective-permute-start.14) | collective-permute-done | bytes 1048608 | tf_op jit(solution)/shard_map/ppermute | solution.py:34
  137.8 0.6 shard_map.89
  138.5 4.1 %collective-permute-start.20 = (f32[32,2048]{1,0:T(8,128)S(1)}, f32[32,2048]{1,0:T(8,128)S(1)}, u32[]{:S(2)}, u32[]{:S(2)}) collective-permute-start(f32[32,2048]{1,0:T(8,128)S(1)} %get-tuple-element.126), channel_id=1, source_target_pairs={{0,16},{1,17},{2,18},{3,19},{4,20},{5,21},{6,22},{7,23},{8,24},{9,... | collective-permute-start | bytes 786440 | tf_op jit(solution)/shard_map/ppermute | solution.py:34
  142.6 0.6 shard_map.90
  143.2 0.6 shard_map.91
  144.0 3.4 %collective-permute-start.26 = (f32[64,1024]{1,0:T(8,128)S(1)}, f32[64,1024]{1,0:T(8,128)S(1)}, u32[]{:S(2)}, u32[]{:S(2)}) collective-permute-start(f32[64,1024]{1,0:T(8,128)S(1)} %get-tuple-element.133), channel_id=1, source_target_pairs={{0,6},{1,7},{2,4},{3,5},{4,2},{5,3},{6,0},{7,1},{8,14},{9,15},{10,... | collective-permute-start | bytes 786440 | tf_op jit(solution)/shard_map/ppermute | solution.py:34
  147.5 4.5 %collective-permute-done.20.refs_1_ = f32[32,2048]{1,0:T(8,128)S(1)} collective-permute-done((f32[32,2048]{1,0:T(8,128)S(1)}, f32[32,2048]{1,0:T(8,128)S(1)}, u32[]{:S(2)}, u32[]{:S(2)}) %collective-permute-start.20) | collective-permute-done | bytes 262176 | tf_op jit(solution)/shard_map/ppermute | solution.py:34
  152.0 6.3 %collective-permute-done.24.refs_1_ = f32[64,1024]{1,0:T(8,128)S(1)} collective-permute-done((f32[64,1024]{1,0:T(8,128)S(1)}, f32[64,1024]{1,0:T(8,128)S(1)}, u32[]{:S(2)}, u32[]{:S(2)}) %collective-permute-start.24) | collective-permute-done | bytes 262176 | tf_op jit(solution)/shard_map/ppermute | solution.py:34
  158.3 3.9 %collective-permute-start.17 = (f32[32,1536]{1,0:T(8,128)S(1)}, f32[32,1536]{1,0:T(8,128)S(1)}, u32[]{:S(2)}, u32[]{:S(2)}) collective-permute-start(f32[32,1536]{1,0:T(8,128)S(1)} %get-tuple-element.123), channel_id=1, source_target_pairs={{0,8},{1,9},{2,10},{3,11},{4,12},{5,13},{6,14},{7,15},{8,0},{9,1},... | collective-permute-start | bytes 589832 | tf_op jit(solution)/shard_map/ppermute | solution.py:34
  162.2 1.5 collective-permute-start.19
  163.7 0.6 shard_map.92
  164.3 2.5 %collective-permute-start.27 = (f32[16,1024]{1,0:T(8,128)S(1)}, f32[16,1024]{1,0:T(8,128)S(1)}, u32[]{:S(2)}, u32[]{:S(2)}) collective-permute-start(f32[16,1024]{1,0:T(8,128)S(1)} %get-tuple-element.137), channel_id=1, source_target_pairs={{0,16},{1,17},{2,18},{3,19},{4,20},{5,21},{6,22},{7,23},{8,24},{9,... | collective-permute-start | bytes 196616 | tf_op jit(solution)/shard_map/ppermute | solution.py:34
  166.8 0.6 shard_map.93
  167.4 2.0 %collective-permute-start.29 = (f32[16,1024]{1,0:T(8,128)S(1)}, f32[16,1024]{1,0:T(8,128)S(1)}, u32[]{:S(2)}, u32[]{:S(2)}) collective-permute-start(f32[16,1024]{1,0:T(8,128)S(1)} %get-tuple-element.139), channel_id=1, source_target_pairs={{0,24},{1,25},{2,26},{3,27},{4,28},{5,29},{6,30},{7,31},{8,16},{9,... | collective-permute-start | bytes 196616 | tf_op jit(solution)/shard_map/ppermute | solution.py:34
  169.5 1.5 collective-permute-done.19.refs_3_
  170.9 0.6 shard_map.94
  171.5 1.2 collective-permute-start.30
  172.7 2.1 %collective-permute-start.31 = (f32[16,2048]{1,0:T(8,128)S(1)}, f32[16,2048]{1,0:T(8,128)S(1)}, u32[]{:S(2)}, u32[]{:S(2)}) collective-permute-start(f32[16,2048]{1,0:T(8,128)S(1)} %get-tuple-element.141), channel_id=1, source_target_pairs={{0,2},{1,3},{2,0},{3,1},{4,6},{5,7},{6,4},{7,5},{8,10},{9,11},{10,... | collective-permute-start | bytes 393224 | tf_op jit(solution)/shard_map/ppermute | solution.py:34
  174.8 1.7 shard_map.95
  176.6 1.0 pad_maximum_fusion
  177.6 0.4 collective-permute-done.30
  178.2 0.7 maximum_multiply_fusion
  (79 shorter events, 1.4 us)
Async XLA Ops:
  5.2 32.0 %collective-permute-start = (f32[224,512]{1,0:T(8,128)}, f32[224,512]{1,0:T(8,128)S(1)}, u32[]{:S(2)}, u32[]{:S(2)}) collective-permute-start(f32[224,512]{1,0:T(8,128)} %get-tuple-element.73.refs_1_), channel_id=1, source_target_pairs={{0,4},{1,5},{2,6},{3,7},{4,0},{5,1},{6,2},{7,3},{8,12},{9,13},{10,... | collective-permute-start | bytes 1376264 | tf_op jit(solution)/shard_map/ppermute | solution.py:29
  8.1 29.0 %collective-permute-start.1 = (f32[224,512]{1,0:T(8,128)}, f32[224,512]{1,0:T(8,128)S(1)}, u32[]{:S(2)}, u32[]{:S(2)}) collective-permute-start(f32[224,512]{1,0:T(8,128)} %get-tuple-element.73.refs_1_), channel_id=1, source_target_pairs={{4,8},{5,9},{6,10},{7,11},{8,4},{9,5},{10,6},{11,7},{12,16},{13,17... | collective-permute-start | bytes 1376264 | tf_op jit(solution)/shard_map/ppermute | solution.py:29
  8.8 8.6 %copy-start.13 = (s32[4]{0:T(128)S(1)}, s32[4]{0:T(128)}, u32[]{:S(2)}) copy-start(s32[4]{0:T(128)} %pad_add_fusion.scalars) | copy-start | bytes 52
  17.4 3.7 %copy-start.1 = (f32[3,3,512,512]{3,2,1,0:T(8,128)S(1)}, f32[3,3,512,512]{3,2,1,0:T(8,128)}, u32[]{:S(2)}) copy-start(f32[3,3,512,512]{3,2,1,0:T(8,128)} %refs_0_.6) | copy-start | bytes 28311556
  21.1 1.2 copy-start.2
  22.3 1.2 copy-start.6
  22.3 1.2 copy-start.11
  22.3 1.3 copy-start.12
  23.6 6.3 %copy-start.10 = (f32[288,512]{1,0:T(8,128)S(1)}, f32[288,512]{1,0:T(8,128)}, u32[]{:S(2)}) copy-start(f32[288,512]{1,0:T(8,128)} %get-tuple-element.84.refs_0_) | copy-start | bytes 1769476
  24.9 38.8 %collective-permute-start.4 = (f32[288,512]{1,0:T(8,128)S(1)}, f32[288,512]{1,0:T(8,128)S(1)}, u32[]{:S(2)}, u32[]{:S(2)}) collective-permute-start(f32[288,512]{1,0:T(8,128)S(1)} %get-tuple-element.85.refs_1_.refs_2_), channel_id=1, source_target_pairs={{0,4},{1,5},{2,6},{3,7},{4,0},{5,1},{6,2},{7,3},{8,12},{9,13},{10,... | collective-permute-start | bytes 1769480 | tf_op jit(solution)/shard_map/ppermute | solution.py:29
  29.2 34.5 %collective-permute-start.5 = (f32[288,512]{1,0:T(8,128)S(1)}, f32[288,512]{1,0:T(8,128)S(1)}, u32[]{:S(2)}, u32[]{:S(2)}) collective-permute-start(f32[288,512]{1,0:T(8,128)S(1)} %get-tuple-element.85.refs_1_.refs_2_), channel_id=1, source_target_pairs={{4,8},{5,9},{6,10},{7,11},{8,4},{9,5},{10,6},{11,7},{12,16},{13,17... | collective-permute-start | bytes 1769480 | tf_op jit(solution)/shard_map/ppermute | solution.py:29
  29.9 1.3 copy-start
  29.9 1.5 copy-start.3
  29.9 1.8 %copy-start.7 = (f32[512,512]{1,0:T(8,128)S(1)}, f32[512,512]{1,0:T(8,128)}, u32[]{:S(2)}) copy-start(f32[512,512]{1,0:T(8,128)} %get-tuple-element.83.refs_2_) | copy-start | bytes 3145732
  31.8 5.4 %copy-start.18 = (f32[224,512]{1,0:T(8,128)S(1)}, f32[224,512]{1,0:T(8,128)}, u32[]{:S(2)}) copy-start(f32[224,512]{1,0:T(8,128)} %get-tuple-element.81.refs_5_) | copy-start | bytes 1376260
  31.8 5.4 %copy-start.19 = (f32[224,512]{1,0:T(8,128)S(1)}, f32[224,512]{1,0:T(8,128)}, u32[]{:S(2)}) copy-start(f32[224,512]{1,0:T(8,128)} %get-tuple-element.82.refs_6_) | copy-start | bytes 1376260
  38.9 24.8 %copy-start.8 = (f32[288,512]{1,0:T(8,128)S(1)}, f32[288,512]{1,0:T(8,128)}, u32[]{:S(2)}) copy-start(f32[288,512]{1,0:T(8,128)} %get-tuple-element.95.refs_5_) | copy-start | bytes 1769476
  39.0 24.7 %copy-start.9 = (f32[288,512]{1,0:T(8,128)S(1)}, f32[288,512]{1,0:T(8,128)}, u32[]{:S(2)}) copy-start(f32[288,512]{1,0:T(8,128)} %get-tuple-element.96.refs_6_) | copy-start | bytes 1769476
  39.0 33.9 %collective-permute-start.2 = (f32[224,512]{1,0:T(8,128)S(1)}, f32[224,512]{1,0:T(8,128)S(1)}, u32[]{:S(2)}, u32[]{:S(2)}) collective-permute-start(f32[224,512]{1,0:T(8,128)S(1)} %get-tuple-element.88.refs_1_.refs_5_), channel_id=1, source_target_pairs={{0,2},{1,3},{2,0},{3,1},{4,6},{5,7},{6,4},{7,5},{8,10},{9,11},{10,... | collective-permute-start | bytes 1376264 | tf_op jit(solution)/shard_map/ppermute | solution.py:29
  40.5 32.9 %collective-permute-start.3 = (f32[224,512]{1,0:T(8,128)S(1)}, f32[224,512]{1,0:T(8,128)S(1)}, u32[]{:S(2)}, u32[]{:S(2)}) collective-permute-start(f32[224,512]{1,0:T(8,128)S(1)} %get-tuple-element.88.refs_1_.refs_5_), channel_id=1, source_target_pairs={{2,4},{3,5},{4,2},{5,3},{6,8},{7,9},{8,6},{9,7},{10,12},{11,13},{1... | collective-permute-start | bytes 1376264 | tf_op jit(solution)/shard_map/ppermute | solution.py:29
  65.5 25.3 %collective-permute-start.8 = (f32[288,512]{1,0:T(8,128)S(1)}, f32[288,512]{1,0:T(8,128)S(1)}, u32[]{:S(2)}, u32[]{:S(2)}) collective-permute-start(f32[288,512]{1,0:T(8,128)S(1)} %get-tuple-element.97.refs_6_.refs_1_), channel_id=1, source_target_pairs={{0,2},{1,3},{2,0},{3,1},{4,6},{5,7},{6,4},{7,5},{8,10},{9,11},{10,... | collective-permute-start | bytes 1769480 | tf_op jit(solution)/shard_map/ppermute | solution.py:29
  67.0 23.8 %collective-permute-start.9 = (f32[288,512]{1,0:T(8,128)S(1)}, f32[288,512]{1,0:T(8,128)S(1)}, u32[]{:S(2)}, u32[]{:S(2)}) collective-permute-start(f32[288,512]{1,0:T(8,128)S(1)} %get-tuple-element.97.refs_6_.refs_1_), channel_id=1, source_target_pairs={{2,4},{3,5},{4,2},{5,3},{6,8},{7,9},{8,6},{9,7},{10,12},{11,13},{1... | collective-permute-start | bytes 1769480 | tf_op jit(solution)/shard_map/ppermute | solution.py:29
  71.2 6.5 %collective-permute-start.10 = (f32[256,1536]{1,0:T(8,128)S(1)}, f32[256,1536]{1,0:T(8,128)S(1)}, u32[]{:S(2)}, u32[]{:S(2)}) collective-permute-start(f32[256,1536]{1,0:T(8,128)S(1)} %get-tuple-element.109), channel_id=1, source_target_pairs={{0,1},{1,0},{2,3},{3,2},{4,5},{5,4},{6,7},{7,6},{8,9},{9,8},{10,11... | collective-permute-start | bytes 4718600 | tf_op jit(solution)/shard_map/ppermute | solution.py:34
  71.3 2.2 %copy-start.16 = (f32[224,512]{1,0:T(8,128)S(1)}, f32[224,512]{1,0:T(8,128)}, u32[]{:S(2)}) copy-start(f32[224,512]{1,0:T(8,128)} %get-tuple-element.92.refs_5_) | copy-start | bytes 1376260
  71.3 2.1 %copy-start.17 = (f32[224,512]{1,0:T(8,128)S(1)}, f32[224,512]{1,0:T(8,128)}, u32[]{:S(2)}) copy-start(f32[224,512]{1,0:T(8,128)} %get-tuple-element.93.refs_6_) | copy-start | bytes 1376260
  72.9 4.8 %collective-permute-start.11 = (f32[256,512]{1,0:T(8,128)S(1)}, f32[256,512]{1,0:T(8,128)S(1)}, u32[]{:S(2)}, u32[]{:S(2)}) collective-permute-start(f32[256,512]{1,0:T(8,128)S(1)} %get-tuple-element.110), channel_id=1, source_target_pairs={{0,1},{1,0},{2,3},{3,2},{4,5},{5,4},{6,7},{7,6},{8,9},{9,8},{10,11... | collective-permute-start | bytes 1572872 | tf_op jit(solution)/shard_map/ppermute | solution.py:34
  76.4 1.3 copy-start.4
  77.7 13.1 %copy-start.14 = (f32[288,512]{1,0:T(8,128)S(1)}, f32[288,512]{1,0:T(8,128)}, u32[]{:S(2)}) copy-start(f32[288,512]{1,0:T(8,128)} %get-tuple-element.107.refs_5_) | copy-start | bytes 1769476
  77.7 13.1 %copy-start.15 = (f32[288,512]{1,0:T(8,128)S(1)}, f32[288,512]{1,0:T(8,128)}, u32[]{:S(2)}) copy-start(f32[288,512]{1,0:T(8,128)} %get-tuple-element.108.refs_6_) | copy-start | bytes 1769476
  95.8 9.2 %collective-permute-start.12 = (f32[256,1536]{1,0:T(8,128)S(1)}, f32[256,1536]{1,0:T(8,128)S(1)}, u32[]{:S(2)}, u32[]{:S(2)}) collective-permute-start(f32[256,1536]{1,0:T(8,128)S(1)} %get-tuple-element.116), channel_id=1, source_target_pairs={{0,1},{1,0},{2,3},{3,2},{4,5},{5,4},{6,7},{7,6},{8,9},{9,8},{10,11... | collective-permute-start | bytes 4718600 | tf_op jit(solution)/shard_map/ppermute | solution.py:34
  95.9 12.7 %collective-permute-start.6 = (f32[224,512]{1,0:T(8,128)S(1)}, f32[224,512]{1,0:T(8,128)S(1)}, u32[]{:S(2)}, u32[]{:S(2)}) collective-permute-start(f32[224,512]{1,0:T(8,128)S(1)} %get-tuple-element.103.refs_1_.refs_5_), channel_id=1, source_target_pairs={{0,1},{1,0},{2,3},{3,2},{4,5},{5,4},{6,7},{7,6},{8,9},{9,8},{10,11... | collective-permute-start | bytes 1376264 | tf_op jit(solution)/shard_map/ppermute | solution.py:29
  96.4 13.9 %collective-permute-start.7 = (f32[224,512]{1,0:T(8,128)S(1)}, f32[224,512]{1,0:T(8,128)S(1)}, u32[]{:S(2)}, u32[]{:S(2)}) collective-permute-start(f32[224,512]{1,0:T(8,128)S(1)} %get-tuple-element.103.refs_1_.refs_5_), channel_id=1, source_target_pairs={{1,2},{2,1},{3,4},{4,3},{5,6},{6,5},{7,8},{8,7},{9,10},{10,9},{11,... | collective-permute-start | bytes 1376264 | tf_op jit(solution)/shard_map/ppermute | solution.py:29
  97.1 13.2 %collective-permute-start.15 = (f32[288,512]{1,0:T(8,128)S(1)}, f32[288,512]{1,0:T(8,128)S(1)}, u32[]{:S(2)}, u32[]{:S(2)}) collective-permute-start(f32[288,512]{1,0:T(8,128)S(1)} %get-tuple-element.112.refs_6_.refs_1_), channel_id=1, source_target_pairs={{0,1},{1,0},{2,3},{3,2},{4,5},{5,4},{6,7},{7,6},{8,9},{9,8},{10,11... | collective-permute-start | bytes 1769480 | tf_op jit(solution)/shard_map/ppermute | solution.py:29
  102.9 7.4 %collective-permute-start.16 = (f32[288,512]{1,0:T(8,128)S(1)}, f32[288,512]{1,0:T(8,128)S(1)}, u32[]{:S(2)}, u32[]{:S(2)}) collective-permute-start(f32[288,512]{1,0:T(8,128)S(1)} %get-tuple-element.112.refs_6_.refs_1_), channel_id=1, source_target_pairs={{1,2},{2,1},{3,4},{4,3},{5,6},{6,5},{7,8},{8,7},{9,10},{10,9},{11,... | collective-permute-start | bytes 1769480 | tf_op jit(solution)/shard_map/ppermute | solution.py:29
  105.1 32.8 %collective-permute-start.14 = (f32[128,2048]{1,0:T(8,128)S(1)}, f32[128,2048]{1,0:T(8,128)S(1)}, u32[]{:S(2)}, u32[]{:S(2)}) collective-permute-start(f32[128,2048]{1,0:T(8,128)S(1)} %get-tuple-element.119), channel_id=1, source_target_pairs={{0,8},{1,9},{2,10},{3,11},{4,12},{5,13},{6,14},{7,15},{8,0},{9,1},... | collective-permute-start | bytes 3145736 | tf_op jit(solution)/shard_map/ppermute | solution.py:34
  108.6 33.9 %collective-permute-start.13 = (f32[128,1536]{1,0:T(8,128)S(1)}, f32[128,1536]{1,0:T(8,128)S(1)}, u32[]{:S(2)}, u32[]{:S(2)}) collective-permute-start(f32[128,1536]{1,0:T(8,128)S(1)} %get-tuple-element.118), channel_id=1, source_target_pairs={{0,4},{1,5},{2,6},{3,7},{4,0},{5,1},{6,2},{7,3},{8,12},{9,13},{10,... | collective-permute-start | bytes 2359304 | tf_op jit(solution)/shard_map/ppermute | solution.py:34
  112.8 30.4 %collective-permute-start.23 = (f32[256,1024]{1,0:T(8,128)S(1)}, f32[256,1024]{1,0:T(8,128)S(1)}, u32[]{:S(2)}, u32[]{:S(2)}) collective-permute-start(f32[256,1024]{1,0:T(8,128)S(1)} %get-tuple-element.129), channel_id=1, source_target_pairs={{0,1},{1,0},{2,3},{3,2},{4,5},{5,4},{6,7},{7,6},{8,9},{9,8},{10,11... | collective-permute-start | bytes 3145736 | tf_op jit(solution)/shard_map/ppermute | solution.py:34
  138.5 13.5 %collective-permute-start.20 = (f32[32,2048]{1,0:T(8,128)S(1)}, f32[32,2048]{1,0:T(8,128)S(1)}, u32[]{:S(2)}, u32[]{:S(2)}) collective-permute-start(f32[32,2048]{1,0:T(8,128)S(1)} %get-tuple-element.126), channel_id=1, source_target_pairs={{0,16},{1,17},{2,18},{3,19},{4,20},{5,21},{6,22},{7,23},{8,24},{9,... | collective-permute-start | bytes 786440 | tf_op jit(solution)/shard_map/ppermute | solution.py:34
  143.9 14.4 %collective-permute-start.24 = (f32[64,1024]{1,0:T(8,128)S(1)}, f32[64,1024]{1,0:T(8,128)S(1)}, u32[]{:S(2)}, u32[]{:S(2)}) collective-permute-start(f32[64,1024]{1,0:T(8,128)S(1)} %get-tuple-element.131), channel_id=1, source_target_pairs={{0,4},{1,5},{2,6},{3,7},{4,0},{5,1},{6,2},{7,3},{8,12},{9,13},{10,... | collective-permute-start | bytes 786440 | tf_op jit(solution)/shard_map/ppermute | solution.py:34
  143.9 18.2 %collective-permute-start.25 = (f32[64,1024]{1,0:T(8,128)S(1)}, f32[64,1024]{1,0:T(8,128)S(1)}, u32[]{:S(2)}, u32[]{:S(2)}) collective-permute-start(f32[64,1024]{1,0:T(8,128)S(1)} %get-tuple-element.132), channel_id=1, source_target_pairs={{0,2},{1,3},{2,0},{3,1},{4,6},{5,7},{6,4},{7,5},{8,10},{9,11},{10,... | collective-permute-start | bytes 786440 | tf_op jit(solution)/shard_map/ppermute | solution.py:34
  144.0 18.2 %collective-permute-start.26 = (f32[64,1024]{1,0:T(8,128)S(1)}, f32[64,1024]{1,0:T(8,128)S(1)}, u32[]{:S(2)}, u32[]{:S(2)}) collective-permute-start(f32[64,1024]{1,0:T(8,128)S(1)} %get-tuple-element.133), channel_id=1, source_target_pairs={{0,6},{1,7},{2,4},{3,5},{4,2},{5,3},{6,0},{7,1},{8,14},{9,15},{10,... | collective-permute-start | bytes 786440 | tf_op jit(solution)/shard_map/ppermute | solution.py:34
  147.4 16.8 %collective-permute-start.21 = (f32[32,2048]{1,0:T(8,128)S(1)}, f32[32,2048]{1,0:T(8,128)S(1)}, u32[]{:S(2)}, u32[]{:S(2)}) collective-permute-start(f32[32,2048]{1,0:T(8,128)S(1)} %get-tuple-element.127), channel_id=1, source_target_pairs={{0,4},{1,5},{2,6},{3,7},{4,0},{5,1},{6,2},{7,3},{8,12},{9,13},{10,... | collective-permute-start | bytes 786440 | tf_op jit(solution)/shard_map/ppermute | solution.py:34
  152.0 14.8 %collective-permute-start.22 = (f32[32,2048]{1,0:T(8,128)S(1)}, f32[32,2048]{1,0:T(8,128)S(1)}, u32[]{:S(2)}, u32[]{:S(2)}) collective-permute-start(f32[32,2048]{1,0:T(8,128)S(1)} %get-tuple-element.128), channel_id=1, source_target_pairs={{0,20},{1,21},{2,22},{3,23},{4,16},{5,17},{6,18},{7,19},{8,28},{9,... | collective-permute-start | bytes 786440 | tf_op jit(solution)/shard_map/ppermute | solution.py:34
  158.3 9.1 %collective-permute-start.17 = (f32[32,1536]{1,0:T(8,128)S(1)}, f32[32,1536]{1,0:T(8,128)S(1)}, u32[]{:S(2)}, u32[]{:S(2)}) collective-permute-start(f32[32,1536]{1,0:T(8,128)S(1)} %get-tuple-element.123), channel_id=1, source_target_pairs={{0,8},{1,9},{2,10},{3,11},{4,12},{5,13},{6,14},{7,15},{8,0},{9,1},... | collective-permute-start | bytes 589832 | tf_op jit(solution)/shard_map/ppermute | solution.py:34
  162.2 7.3 %collective-permute-start.18 = (f32[32,1536]{1,0:T(8,128)S(1)}, f32[32,1536]{1,0:T(8,128)S(1)}, u32[]{:S(2)}, u32[]{:S(2)}) collective-permute-start(f32[32,1536]{1,0:T(8,128)S(1)} %get-tuple-element.124), channel_id=1, source_target_pairs={{0,2},{1,3},{2,0},{3,1},{4,6},{5,7},{6,4},{7,5},{8,10},{9,11},{10,... | collective-permute-start | bytes 589832 | tf_op jit(solution)/shard_map/ppermute | solution.py:34
  162.2 8.7 %collective-permute-start.19 = (f32[32,1536]{1,0:T(8,128)S(1)}, f32[32,1536]{1,0:T(8,128)S(1)}, u32[]{:S(2)}, u32[]{:S(2)}) collective-permute-start(f32[32,1536]{1,0:T(8,128)S(1)} %get-tuple-element.125), channel_id=1, source_target_pairs={{0,10},{1,11},{2,8},{3,9},{4,14},{5,15},{6,12},{7,13},{8,2},{9,3},... | collective-permute-start | bytes 589832 | tf_op jit(solution)/shard_map/ppermute | solution.py:34
  164.3 13.3 %collective-permute-start.27 = (f32[16,1024]{1,0:T(8,128)S(1)}, f32[16,1024]{1,0:T(8,128)S(1)}, u32[]{:S(2)}, u32[]{:S(2)}) collective-permute-start(f32[16,1024]{1,0:T(8,128)S(1)} %get-tuple-element.137), channel_id=1, source_target_pairs={{0,16},{1,17},{2,18},{3,19},{4,20},{5,21},{6,22},{7,23},{8,24},{9,... | collective-permute-start | bytes 196616 | tf_op jit(solution)/shard_map/ppermute | solution.py:34
  166.8 10.8 %collective-permute-start.28 = (f32[16,1024]{1,0:T(8,128)S(1)}, f32[16,1024]{1,0:T(8,128)S(1)}, u32[]{:S(2)}, u32[]{:S(2)}) collective-permute-start(f32[16,1024]{1,0:T(8,128)S(1)} %get-tuple-element.138), channel_id=1, source_target_pairs={{0,8},{1,9},{2,10},{3,11},{4,12},{5,13},{6,14},{7,15},{8,0},{9,1},... | collective-permute-start | bytes 196616 | tf_op jit(solution)/shard_map/ppermute | solution.py:34
  167.4 10.2 %collective-permute-start.29 = (f32[16,1024]{1,0:T(8,128)S(1)}, f32[16,1024]{1,0:T(8,128)S(1)}, u32[]{:S(2)}, u32[]{:S(2)}) collective-permute-start(f32[16,1024]{1,0:T(8,128)S(1)} %get-tuple-element.139), channel_id=1, source_target_pairs={{0,24},{1,25},{2,26},{3,27},{4,28},{5,29},{6,30},{7,31},{8,16},{9,... | collective-permute-start | bytes 196616 | tf_op jit(solution)/shard_map/ppermute | solution.py:34
  170.9 3.9 %copy-start.5 = (f32[224,512]{1,0:T(8,128)S(1)}, f32[224,512]{1,0:T(8,128)}, u32[]{:S(2)}) copy-start(f32[224,512]{1,0:T(8,128)} %copy-done.4) | copy-start | bytes 1376260
  171.5 6.6 %collective-permute-start.30 = (f32[16,1536]{1,0:T(8,128)S(1)}, f32[16,1536]{1,0:T(8,128)S(1)}, u32[]{:S(2)}, u32[]{:S(2)}) collective-permute-start(f32[16,1536]{1,0:T(8,128)S(1)} %get-tuple-element.140), channel_id=1, source_target_pairs={{0,16},{1,17},{2,18},{3,19},{4,20},{5,21},{6,22},{7,23},{8,24},{9,... | collective-permute-start | bytes 294920 | tf_op jit(solution)/shard_map/ppermute | solution.py:34
  172.7 5.4 %collective-permute-start.31 = (f32[16,2048]{1,0:T(8,128)S(1)}, f32[16,2048]{1,0:T(8,128)S(1)}, u32[]{:S(2)}, u32[]{:S(2)}) collective-permute-start(f32[16,2048]{1,0:T(8,128)S(1)} %get-tuple-element.141), channel_id=1, source_target_pairs={{0,2},{1,3},{2,0},{3,1},{4,6},{5,7},{6,4},{7,5},{8,10},{9,11},{10,... | collective-permute-start | bytes 393224 | tf_op jit(solution)/shard_map/ppermute | solution.py:34

commit v3 on v2

--- a/solution.py
+++ b/solution.py
@@ -13,10 +13,10 @@
 F32 = jnp.float32
 STRIP = 32
 PIECES = (2,)
-GROUPS = (((0,), (1, 2), (3, 4)), ((0,), (2,), (1, 3), (4,)), ((0,), (3,), (2, 4), (1,)))
-FIRST_SIXTEENTHS = 7
+GROUPS = (((0,), (1, 2), (3, 4)), ((0,), (1,), (3,), (4,), (2,)), ((0,), (3,), (2, 4), (1,)))
+FIRST_SIXTEENTHS = 8
 UNIT = 5 * 10**9
-ORDER = (('top', 0), ('prep', 0), ('w', 6), ('ca2', 1), ('cb2', 6), ('turn', 2), ('aa2', 1), ('ca1', 4), ('ab2', 0), ('t2', 1), ('m2', 2), ('aa1', 3), ('ca0', 0), ('cb1', 0), ('r2', 0), ('ab1', 1), ('t1', 10), ('cb0', 1), ('r1', 3), ('t0', 6), ('ab0', 0), ('r2', 4), ('r1', 0), ('r0', 0), ('r0', 0), ('r2', 0), ('r1', 6), ('aa0', 1))
+ORDER = (('top', 4), ('prep', 6), ('w', 1), ('ca2', 0), ('turn', 0), ('aa2', 4), ('ca1', 1), ('cb2', 0), ('ab2', 1), ('cb1', 3), ('m2', 4), ('t2', 4), ('aa1', 10), ('r2', 0), ('ab1', 2), ('t1', 0), ('r2', 3), ('r1', 10), ('ca0', 4), ('cb0', 6), ('aa0', 0), ('t0', 1), ('r1', 4), ('r2', 3), ('r0', 0), ('r1', 0), ('ab0', 0), ('r0', 6), ('r1', 0))
 
 
 def paired(array, jump, parity):

time: 179 us -> 175 us (0.978)
  starting transfers between devices: 63.2 us -> 54.9 us
  waiting for transfers between devices: 53.7 us -> 58.5 us
    ppermute x20 -> x19, waiting for transfers between devices: 20.2 us -> 31.3 us  [swapped(): return lax.ppermute(array, 'seq', [(i, i ^ mask) for i in range(devices)])]
    ppermute x20 -> x19, starting transfers between devices: 42 us -> 33.8 us  [swapped(): return lax.ppermute(array, 'seq', [(i, i ^ mask) for i in range(devices)])]
    ppermute x12, waiting for transfers between devices: 33.5 us -> 27.3 us  [paired(): return lax.ppermute(array, 'seq', pairs)]
    pallas_call x28 -> x29, Pallas kernels: 52.4 us -> 52.4 us  [__call__(): pl.pallas_call(kernel, grid_spec=pltpu.PrefetchScalarGridSpec(num_scalar_...]
  transfers between devices with their start and end apart: 32 -> 31, of which waited for: 8 -> 12; matrix products, arithmetic and copies ran while one was open for 1% -> 1% of each run, Pallas kernels for 24% -> 28%
where the time goes in v3:
time: 175 us
  waiting for transfers between devices  58.5 us (33%)
  starting transfers between devices  54.9 us (31%)
  Pallas kernels  52.4 us (30%)
  local copies, waits for them, and re-layouts  5.18 us (3%)
  other arithmetic  2.51 us (1%)
    pallas_call x29, Pallas kernels, __call__(): pl.pallas_call(kernel, grid_spec=pltpu.PrefetchScalarGridSpec(num_scalar_...  52.4 us
    ppermute x19, starting transfers between devices, swapped(): return lax.ppermute(array, 'seq', [(i, i ^ mask) for i in range(devices)])  33.8 us
    ppermute x19, waiting for transfers between devices, swapped(): return lax.ppermute(array, 'seq', [(i, i ^ mask) for i in range(devices)])  31.3 us
    ppermute x12, waiting for transfers between devices, paired(): return lax.ppermute(array, 'seq', pairs)  27.3 us
    ppermute x12, starting transfers between devices, paired(): return lax.ppermute(array, 'seq', pairs)  21.2 us
    unnamed x40, local copies, waits for them, and re-layouts  5.15 us
  transfers between devices with their start and end apart: 31, of which 12 were waited for; matrix products, arithmetic and copies ran while one was open for 1% of the time, Pallas kernels for 28%

profile of v3, /device:TPU:0, one launch (start us, length us, event | category | flops | bytes accessed | tf_op | source)
XLA Modules:
  0.0 174.8 jit_solution(2557499182670656154)
XLA Ops:
  0.7 0.7 pad_add_fusion.scalars
  1.4 4.1 %shard_map.68 = (f32[256,512]{1,0:T(8,128)}, f32[256,512]{1,0:T(8,128)}) custom-call(s32[4]{0:T(128)} %pad_add_fusion.scalars, f32[512,512]{1,0:T(8,128)} %refs_0_.7, f32[3,512,512]{2,1,0:T(8,128)} %refs_1_.3, f32[3,512,512]{2,1,0:T(8,128)} %refs_1_.3, f32[3,512,512]{2,1,0:T(8,128)} %refs_1_.3, f32[3,512,512]{2,1,0:T(8,128)} %refs_2_.3, f32[512,512]{1,0:T(8,128)} %refs_3_.3), custom_call_target="tpu_custom_call" | custom-call | bytes 1024 | tf_op jit(solution)/shard_map/pallas_call | solution.py:73
  5.4 3.0 %collective-permute-start = (f32[256,512]{1,0:T(8,128)}, f32[256,512]{1,0:T(8,128)S(1)}, u32[]{:S(2)}, u32[]{:S(2)}) collective-permute-start(f32[256,512]{1,0:T(8,128)} %get-tuple-element.73.refs_1_), channel_id=1, source_target_pairs={{0,4},{1,5},{2,6},{3,7},{4,0},{5,1},{6,2},{7,3},{8,12},{9,13},{10,... | collective-permute-start | bytes 1572872 | tf_op jit(solution)/shard_map/ppermute | solution.py:29
  8.4 0.7 collective-permute-start.1
  9.1 8.5 %shard_map.69 = (f32[512,512]{1,0:T(8,128)}, f32[512,512]{1,0:T(8,128)}, f32[256,512]{1,0:T(8,128)}, f32[256,512]{1,0:T(8,128)}, f32[256,512]{1,0:T(8,128)}, /*i...) custom-call(s32[4]{0:T(128)} %pad_add_fusion.scalars, ...), custom_call_target="tpu_custom_call" | custom-call | bytes 1024 | tf_op jit(solution)/shard_map/pallas_call | solution.py:73
  17.6 3.7 %copy-done.1 = f32[3,3,512,512]{3,2,1,0:T(8,128)S(1)} copy-done((f32[3,3,512,512]{3,2,1,0:T(8,128)S(1)}, f32[3,3,512,512]{3,2,1,0:T(8,128)}, u32[]{:S(2)}) %copy-start.1) | copy-done | bytes 9437208
  21.3 1.2 copy-done.2
  22.5 1.1 shard_map.70
  23.9 1.2 shard_map.71
  25.1 4.3 %collective-permute-start.4 = (f32[256,512]{1,0:T(8,128)S(1)}, f32[256,512]{1,0:T(8,128)S(1)}, u32[]{:S(2)}, u32[]{:S(2)}) collective-permute-start(f32[256,512]{1,0:T(8,128)S(1)} %get-tuple-element.93.refs_1_.refs_2_), channel_id=1, source_target_pairs={{0,4},{1,5},{2,6},{3,7},{4,0},{5,1},{6,2},{7,3},{8,12},{9,13},{10,... | collective-permute-start | bytes 1572872 | tf_op jit(solution)/shard_map/ppermute | solution.py:29
  29.4 0.7 collective-permute-start.5
  30.1 5.4 %shard_map.72 = (f32[512,512]{1,0:T(8,128)S(1)}, f32[512,512]{1,0:T(8,128)S(1)}, f32[512,512]{1,0:T(8,128)S(1)}, f32[512,512]{1,0:T(8,128)S(1)}, f32[512,512]{1,0:T(8,128)S(1)}) custom-call(s32[4]{0:T(128)S(1)} %copy-done.9, f32[512,512]{1,0:T(8,128)S(1)} %copy-done, f32[512,512]{1,0:T(8,128)S(1)} %copy-done.3, f32[512,512]{1,0:T(8,128)S(1)} %copy-done.5, ...), custom_call_target="tpu_custom_call" | custom-call | bytes 1024 | tf_op jit(solution)/shard_map/pallas_call | solution.py:73
  35.5 7.9 %collective-permute-done.refs_1_ = f32[256,512]{1,0:T(8,128)S(1)} collective-permute-done((f32[256,512]{1,0:T(8,128)}, f32[256,512]{1,0:T(8,128)S(1)}, u32[]{:S(2)}, u32[]{:S(2)}) %collective-permute-start) | collective-permute-done | bytes 524320 | tf_op jit(solution)/shard_map/ppermute | solution.py:29
  43.4 1.6 shard_map.73
  45.0 1.6 collective-permute-start.2
  46.6 0.7 collective-permute-start.3
  47.3 1.2 shard_map.74.refs_3_.refs_0_
  48.5 1.2 shard_map.75.refs_0_.refs_7_
  49.7 15.0 %collective-permute-done.4.refs_1_.refs_3_ = f32[256,512]{1,0:T(8,128)S(1)} collective-permute-done((f32[256,512]{1,0:T(8,128)S(1)}, f32[256,512]{1,0:T(8,128)S(1)}, u32[]{:S(2)}, u32[]{:S(2)}) %collective-permute-start.4) | collective-permute-done | bytes 524320 | tf_op jit(solution)/shard_map/ppermute | solution.py:29
  64.7 1.6 shard_map.76
  66.4 1.6 collective-permute-start.6
  67.9 0.9 collective-permute-start.7
  68.8 1.2 shard_map.77.refs_3_.refs_0_
  70.0 1.6 shard_map.78
  71.6 3.3 %shard_map.79 = (f32[256,1536]{1,0:T(8,128)S(1)}, f32[256,1536]{1,0:T(8,128)S(1)}) custom-call(s32[4]{0:T(128)S(1)} %copy-done.9, f32[512,512]{1,0:T(8,128)S(1)} %get-tuple-element.92.refs_0_, f32[256,512]{1,0:T(8,128)S(1)} %collective-permute-done.refs_1_, f32[256,512]{1,0:T(8,128)S(1)} %collective-permute-done.1.refs_2_, ...), custom_call_target="tpu_custom_call" | custom-call | flops 20000000000 | bytes 1024 | tf_op jit(solution)/shard_map/pallas_call | solution.py:73
  75.5 1.7 shard_map.80
  77.2 2.0 %collective-permute-done.8.refs_2_ = f32[256,512]{1,0:T(8,128)S(1)} collective-permute-done((f32[256,512]{1,0:T(8,128)S(1)}, f32[256,512]{1,0:T(8,128)S(1)}, u32[]{:S(2)}, u32[]{:S(2)}) %collective-permute-start.8) | collective-permute-done | bytes 524320 | tf_op jit(solution)/shard_map/ppermute | solution.py:34
  79.2 0.8 shard_map.81
  79.9 5.2 %collective-permute-start.11 = (f32[128,2048]{1,0:T(8,128)S(1)}, f32[128,2048]{1,0:T(8,128)S(1)}, u32[]{:S(2)}, u32[]{:S(2)}) collective-permute-start(f32[128,2048]{1,0:T(8,128)S(1)} %get-tuple-element.116), channel_id=1, source_target_pairs={{0,8},{1,9},{2,10},{3,11},{4,12},{5,13},{6,14},{7,15},{8,0},{9,1},... | collective-permute-start | bytes 3145736 | tf_op jit(solution)/shard_map/ppermute | solution.py:34
  85.1 4.4 %collective-permute-done.6.refs_1_.refs_3_ = f32[256,512]{1,0:T(8,128)S(1)} collective-permute-done((f32[256,512]{1,0:T(8,128)S(1)}, f32[256,512]{1,0:T(8,128)S(1)}, u32[]{:S(2)}, u32[]{:S(2)}) %collective-permute-start.6) | collective-permute-done | bytes 524320 | tf_op jit(solution)/shard_map/ppermute | solution.py:29
  89.5 1.6 shard_map.82
  91.2 3.3 %shard_map.83 = (f32[256,1536]{1,0:T(8,128)S(1)}, f32[256,1536]{1,0:T(8,128)S(1)}) custom-call(s32[4]{0:T(128)S(1)} %copy-done.9, f32[512,512]{1,0:T(8,128)S(1)} %get-tuple-element.105.refs_0_, f32[256,512]{1,0:T(8,128)S(1)} %collective-permute-done.2.refs_1_, f32[256,512]{1,0:T(8,128)S(1)} %collective-permute-done.3.refs_2_, ...), custom_call_target="tpu_custom_call" | custom-call | bytes 1024 | tf_op jit(solution)/shard_map/pallas_call | solution.py:73
  95.1 0.7 collective-permute-start.13
  95.8 5.8 %collective-permute-start.14 = (f32[256,512]{1,0:T(8,128)S(1)}, f32[256,512]{1,0:T(8,128)S(1)}, u32[]{:S(2)}, u32[]{:S(2)}) collective-permute-start(f32[256,512]{1,0:T(8,128)S(1)} %get-tuple-element.111.refs_6_.refs_1_), channel_id=1, source_target_pairs={{0,1},{1,0},{2,3},{3,2},{4,5},{5,4},{6,7},{7,6},{8,9},{9,8},{10,11... | collective-permute-start | bytes 1572872 | tf_op jit(solution)/shard_map/ppermute | solution.py:29
  101.5 7.0 %collective-permute-done.11.refs_1_ = f32[128,2048]{1,0:T(8,128)S(1)} collective-permute-done((f32[128,2048]{1,0:T(8,128)S(1)}, f32[128,2048]{1,0:T(8,128)S(1)}, u32[]{:S(2)}, u32[]{:S(2)}) %collective-permute-start.11) | collective-permute-done | bytes 1048608 | tf_op jit(solution)/shard_map/ppermute | solution.py:34
  108.6 0.9 collective-permute-start.15
  109.5 0.6 shard_map.84
  110.2 0.7 shard_map.85
  110.9 3.1 %collective-permute-start.16 = (f32[128,1536]{1,0:T(8,128)S(1)}, f32[128,1536]{1,0:T(8,128)S(1)}, u32[]{:S(2)}, u32[]{:S(2)}) collective-permute-start(f32[128,1536]{1,0:T(8,128)S(1)} %get-tuple-element.120), channel_id=1, source_target_pairs={{0,2},{1,3},{2,0},{3,1},{4,6},{5,7},{6,4},{7,5},{8,10},{9,11},{10,... | collective-permute-start | bytes 2359304 | tf_op jit(solution)/shard_map/ppermute | solution.py:34
  113.9 1.2 shard_map.86.refs_3_.refs_0_
  115.1 1.2 shard_map.87.refs_5_.refs_0_
  116.3 2.7 %collective-permute-start.19 = (f32[32,2048]{1,0:T(8,128)S(1)}, f32[32,2048]{1,0:T(8,128)S(1)}, u32[]{:S(2)}, u32[]{:S(2)}) collective-permute-start(f32[32,2048]{1,0:T(8,128)S(1)} %get-tuple-element.125), channel_id=1, source_target_pairs={{0,16},{1,17},{2,18},{3,19},{4,20},{5,21},{6,22},{7,23},{8,24},{9,... | collective-permute-start | bytes 786440 | tf_op jit(solution)/shard_map/ppermute | solution.py:34
  119.4 1.6 shard_map.88.refs_5_
  121.0 1.5 collective-permute-start.21
  122.5 2.4 %shard_map.89 = (f32[256,1024]{1,0:T(8,128)S(1)}, f32[256,1024]{1,0:T(8,128)S(1)}) custom-call(s32[4]{0:T(128)S(1)} %copy-done.9, f32[512,512]{1,0:T(8,128)S(1)} %copy-done.11, f32[256,512]{1,0:T(8,128)S(1)} %collective-permute-done.12.refs_1_, f32[256,512]{1,0:T(8,128)S(1)} %collective-permute-done.13.refs_2_, ...), custom_call_target="tpu_custom_call" | custom-call | flops 5000000000 | bytes 1024 | tf_op jit(solution)/shard_map/pallas_call | solution.py:73
  124.9 6.6 %collective-permute-start.18 = (f32[256,1024]{1,0:T(8,128)S(1)}, f32[256,1024]{1,0:T(8,128)S(1)}, u32[]{:S(2)}, u32[]{:S(2)}) collective-permute-start(f32[256,1024]{1,0:T(8,128)S(1)} %get-tuple-element.124), channel_id=1, source_target_pairs={{0,1},{1,0},{2,3},{3,2},{4,5},{5,4},{6,7},{7,6},{8,9},{9,8},{10,11... | collective-permute-start | bytes 3145736 | tf_op jit(solution)/shard_map/ppermute | solution.py:34
  131.6 10.0 %collective-permute-done.16.refs_1_ = f32[128,1536]{1,0:T(8,128)S(1)} collective-permute-done((f32[128,1536]{1,0:T(8,128)S(1)}, f32[128,1536]{1,0:T(8,128)S(1)}, u32[]{:S(2)}, u32[]{:S(2)}) %collective-permute-start.16) | collective-permute-done | bytes 786464 | tf_op jit(solution)/shard_map/ppermute | solution.py:34
  141.6 0.6 shard_map.90
  142.2 2.2 %collective-permute-start.17 = (f32[64,1536]{1,0:T(8,128)S(1)}, f32[64,1536]{1,0:T(8,128)S(1)}, u32[]{:S(2)}, u32[]{:S(2)}) collective-permute-start(f32[64,1536]{1,0:T(8,128)S(1)} %get-tuple-element.123), channel_id=1, source_target_pairs={{0,8},{1,9},{2,10},{3,11},{4,12},{5,13},{6,14},{7,15},{8,0},{9,1},... | collective-permute-start | bytes 1179656 | tf_op jit(solution)/shard_map/ppermute | solution.py:34
  145.1 0.7 collective-permute-start.30
  145.8 0.6 shard_map.92
  146.4 1.3 collective-permute-start.22
  147.7 2.0 %collective-permute-start.23 = (f32[64,1024]{1,0:T(8,128)S(1)}, f32[64,1024]{1,0:T(8,128)S(1)}, u32[]{:S(2)}, u32[]{:S(2)}) collective-permute-start(f32[64,1024]{1,0:T(8,128)S(1)} %get-tuple-element.132), channel_id=1, source_target_pairs={{0,2},{1,3},{2,0},{3,1},{4,6},{5,7},{6,4},{7,5},{8,10},{9,11},{10,... | collective-permute-start | bytes 786440 | tf_op jit(solution)/shard_map/ppermute | solution.py:34
  150.0 1.2 collective-permute-done.30
  151.2 2.6 %collective-permute-done.17.refs_1_ = f32[64,1536]{1,0:T(8,128)S(1)} collective-permute-done((f32[64,1536]{1,0:T(8,128)S(1)}, f32[64,1536]{1,0:T(8,128)S(1)}, u32[]{:S(2)}, u32[]{:S(2)}) %collective-permute-start.17) | collective-permute-done | bytes 393248 | tf_op jit(solution)/shard_map/ppermute | solution.py:34
  154.4 2.3 %collective-permute-start.28 = (f32[32,1536]{1,0:T(8,128)S(1)}, f32[32,1536]{1,0:T(8,128)S(1)}, u32[]{:S(2)}, u32[]{:S(2)}) collective-permute-start(f32[32,1536]{1,0:T(8,128)S(1)} %get-tuple-element.138), channel_id=1, source_target_pairs={{0,16},{1,17},{2,18},{3,19},{4,20},{5,21},{6,22},{7,23},{8,24},{9,... | collective-permute-start | bytes 589832 | tf_op jit(solution)/shard_map/ppermute | solution.py:34
  156.7 1.6 shard_map.94.refs_4_
  158.4 4.2 %collective-permute-done.24.refs_3_ = f32[64,1024]{1,0:T(8,128)S(1)} collective-permute-done((f32[64,1024]{1,0:T(8,128)S(1)}, f32[64,1024]{1,0:T(8,128)S(1)}, u32[]{:S(2)}, u32[]{:S(2)}) %collective-permute-start.24) | collective-permute-done | bytes 262176 | tf_op jit(solution)/shard_map/ppermute | solution.py:34
  163.5 2.1 %collective-permute-start.26 = (f32[16,1024]{1,0:T(8,128)S(1)}, f32[16,1024]{1,0:T(8,128)S(1)}, u32[]{:S(2)}, u32[]{:S(2)}) collective-permute-start(f32[16,1024]{1,0:T(8,128)S(1)} %get-tuple-element.136), channel_id=1, source_target_pairs={{0,8},{1,9},{2,10},{3,11},{4,12},{5,13},{6,14},{7,15},{8,0},{9,1},... | collective-permute-start | bytes 196616 | tf_op jit(solution)/shard_map/ppermute | solution.py:34
  165.6 2.1 %collective-permute-start.27 = (f32[16,1024]{1,0:T(8,128)S(1)}, f32[16,1024]{1,0:T(8,128)S(1)}, u32[]{:S(2)}, u32[]{:S(2)}) collective-permute-start(f32[16,1024]{1,0:T(8,128)S(1)} %get-tuple-element.137), channel_id=1, source_target_pairs={{0,24},{1,25},{2,26},{3,27},{4,28},{5,29},{6,30},{7,31},{8,16},{9,... | collective-permute-start | bytes 196616 | tf_op jit(solution)/shard_map/ppermute | solution.py:34
  167.7 1.0 pad_maximum_fusion
  170.2 1.5 collective-permute-done.27
  171.7 2.3 %collective-permute-done.29 = f32[16,1536]{1,0:T(8,128)S(1)} collective-permute-done((f32[16,1536]{1,0:T(8,128)S(1)}, f32[16,1536]{1,0:T(8,128)S(1)}, u32[]{:S(2)}, u32[]{:S(2)}) %collective-permute-start.29) | collective-permute-done | bytes 98336 | tf_op jit(solution)/shard_map/ppermute | solution.py:34
  174.1 0.7 maximum_multiply_fusion
  (78 shorter events, 5.6 us)
Async XLA Ops:
  5.4 37.9 %collective-permute-start = (f32[256,512]{1,0:T(8,128)}, f32[256,512]{1,0:T(8,128)S(1)}, u32[]{:S(2)}, u32[]{:S(2)}) collective-permute-start(f32[256,512]{1,0:T(8,128)} %get-tuple-element.73.refs_1_), channel_id=1, source_target_pairs={{0,4},{1,5},{2,6},{3,7},{4,0},{5,1},{6,2},{7,3},{8,12},{9,13},{10,... | collective-permute-start | bytes 1572872 | tf_op jit(solution)/shard_map/ppermute | solution.py:29
  8.4 35.0 %collective-permute-start.1 = (f32[256,512]{1,0:T(8,128)}, f32[256,512]{1,0:T(8,128)S(1)}, u32[]{:S(2)}, u32[]{:S(2)}) collective-permute-start(f32[256,512]{1,0:T(8,128)} %get-tuple-element.73.refs_1_), channel_id=1, source_target_pairs={{4,8},{5,9},{6,10},{7,11},{8,4},{9,5},{10,6},{11,7},{12,16},{13,17... | collective-permute-start | bytes 1572872 | tf_op jit(solution)/shard_map/ppermute | solution.py:29
  9.1 8.5 %copy-start.9 = (s32[4]{0:T(128)S(1)}, s32[4]{0:T(128)}, u32[]{:S(2)}) copy-start(s32[4]{0:T(128)} %pad_add_fusion.scalars) | copy-start | bytes 52
  17.6 3.7 %copy-start.1 = (f32[3,3,512,512]{3,2,1,0:T(8,128)S(1)}, f32[3,3,512,512]{3,2,1,0:T(8,128)}, u32[]{:S(2)}) copy-start(f32[3,3,512,512]{3,2,1,0:T(8,128)} %refs_0_.6) | copy-start | bytes 28311556
  21.3 1.2 copy-start.2
  22.5 1.2 copy-start.4
  22.5 1.2 copy-start.6
  22.5 1.4 copy-start.8
  23.9 6.2 %copy-start = (f32[512,512]{1,0:T(8,128)S(1)}, f32[512,512]{1,0:T(8,128)}, u32[]{:S(2)}) copy-start(f32[512,512]{1,0:T(8,128)} %refs_0_.7) | copy-start | bytes 3145732
  23.9 6.2 %copy-start.3 = (f32[512,512]{1,0:T(8,128)S(1)}, f32[512,512]{1,0:T(8,128)}, u32[]{:S(2)}) copy-start(f32[512,512]{1,0:T(8,128)} %get-tuple-element.74.refs_1_) | copy-start | bytes 3145732
  23.9 6.2 %copy-start.5 = (f32[512,512]{1,0:T(8,128)S(1)}, f32[512,512]{1,0:T(8,128)}, u32[]{:S(2)}) copy-start(f32[512,512]{1,0:T(8,128)} %get-tuple-element.83.refs_2_) | copy-start | bytes 3145732
  25.1 39.7 %collective-permute-start.4 = (f32[256,512]{1,0:T(8,128)S(1)}, f32[256,512]{1,0:T(8,128)S(1)}, u32[]{:S(2)}, u32[]{:S(2)}) collective-permute-start(f32[256,512]{1,0:T(8,128)S(1)} %get-tuple-element.93.refs_1_.refs_2_), channel_id=1, source_target_pairs={{0,4},{1,5},{2,6},{3,7},{4,0},{5,1},{6,2},{7,3},{8,12},{9,13},{10,... | collective-permute-start | bytes 1572872 | tf_op jit(solution)/shard_map/ppermute | solution.py:29
  29.4 35.4 %collective-permute-start.5 = (f32[256,512]{1,0:T(8,128)S(1)}, f32[256,512]{1,0:T(8,128)S(1)}, u32[]{:S(2)}, u32[]{:S(2)}) collective-permute-start(f32[256,512]{1,0:T(8,128)S(1)} %get-tuple-element.93.refs_1_.refs_2_), channel_id=1, source_target_pairs={{4,8},{5,9},{6,10},{7,11},{8,4},{9,5},{10,6},{11,7},{12,16},{13,17... | collective-permute-start | bytes 1572872 | tf_op jit(solution)/shard_map/ppermute | solution.py:29
  30.1 13.3 %copy-start.18 = (f32[256,512]{1,0:T(8,128)S(1)}, f32[256,512]{1,0:T(8,128)}, u32[]{:S(2)}) copy-start(f32[256,512]{1,0:T(8,128)} %get-tuple-element.81.refs_5_) | copy-start | bytes 1572868
  30.1 13.3 %copy-start.19 = (f32[256,512]{1,0:T(8,128)S(1)}, f32[256,512]{1,0:T(8,128)}, u32[]{:S(2)}) copy-start(f32[256,512]{1,0:T(8,128)} %get-tuple-element.82.refs_6_) | copy-start | bytes 1572868
  35.5 9.5 %copy-start.10 = (f32[512,512]{1,0:T(8,128)}, f32[512,512]{1,0:T(8,128)S(1)}, u32[]{:S(2)}) copy-start(f32[512,512]{1,0:T(8,128)S(1)} %get-tuple-element.84.refs_7_.refs_0_) | copy-start | bytes 3145732
  45.0 30.0 %collective-permute-start.2 = (f32[256,512]{1,0:T(8,128)S(1)}, f32[256,512]{1,0:T(8,128)S(1)}, u32[]{:S(2)}, u32[]{:S(2)}) collective-permute-start(f32[256,512]{1,0:T(8,128)S(1)} %get-tuple-element.86.refs_1_.refs_5_), channel_id=1, source_target_pairs={{0,2},{1,3},{2,0},{3,1},{4,6},{5,7},{6,4},{7,5},{8,10},{9,11},{10,... | collective-permute-start | bytes 1572872 | tf_op jit(solution)/shard_map/ppermute | solution.py:29
  46.6 28.9 %collective-permute-start.3 = (f32[256,512]{1,0:T(8,128)S(1)}, f32[256,512]{1,0:T(8,128)S(1)}, u32[]{:S(2)}, u32[]{:S(2)}) collective-permute-start(f32[256,512]{1,0:T(8,128)S(1)} %get-tuple-element.86.refs_1_.refs_5_), channel_id=1, source_target_pairs={{2,4},{3,5},{4,2},{5,3},{6,8},{7,9},{8,6},{9,7},{10,12},{11,13},{1... | collective-permute-start | bytes 1572872 | tf_op jit(solution)/shard_map/ppermute | solution.py:29
  47.3 1.2 copy-start.7
  48.5 16.2 %copy-start.16 = (f32[256,512]{1,0:T(8,128)S(1)}, f32[256,512]{1,0:T(8,128)}, u32[]{:S(2)}) copy-start(f32[256,512]{1,0:T(8,128)} %get-tuple-element.95.refs_5_) | copy-start | bytes 1572868
  48.5 16.2 %copy-start.17 = (f32[256,512]{1,0:T(8,128)S(1)}, f32[256,512]{1,0:T(8,128)}, u32[]{:S(2)}) copy-start(f32[256,512]{1,0:T(8,128)} %get-tuple-element.96.refs_6_) | copy-start | bytes 1572868
  66.4 23.1 %collective-permute-start.6 = (f32[256,512]{1,0:T(8,128)S(1)}, f32[256,512]{1,0:T(8,128)S(1)}, u32[]{:S(2)}, u32[]{:S(2)}) collective-permute-start(f32[256,512]{1,0:T(8,128)S(1)} %get-tuple-element.97.refs_1_.refs_6_), channel_id=1, source_target_pairs={{0,2},{1,3},{2,0},{3,1},{4,6},{5,7},{6,4},{7,5},{8,10},{9,11},{10,... | collective-permute-start | bytes 1572872 | tf_op jit(solution)/shard_map/ppermute | solution.py:29
  67.9 21.6 %collective-permute-start.7 = (f32[256,512]{1,0:T(8,128)S(1)}, f32[256,512]{1,0:T(8,128)S(1)}, u32[]{:S(2)}, u32[]{:S(2)}) collective-permute-start(f32[256,512]{1,0:T(8,128)S(1)} %get-tuple-element.97.refs_1_.refs_6_), channel_id=1, source_target_pairs={{2,4},{3,5},{4,2},{5,3},{6,8},{7,9},{8,6},{9,7},{10,12},{11,13},{1... | collective-permute-start | bytes 1572872 | tf_op jit(solution)/shard_map/ppermute | solution.py:29
  71.6 3.9 %copy-start.14 = (f32[256,512]{1,0:T(8,128)S(1)}, f32[256,512]{1,0:T(8,128)}, u32[]{:S(2)}) copy-start(f32[256,512]{1,0:T(8,128)} %get-tuple-element.90.refs_5_) | copy-start | bytes 1572868
  71.6 3.9 %copy-start.15 = (f32[256,512]{1,0:T(8,128)S(1)}, f32[256,512]{1,0:T(8,128)}, u32[]{:S(2)}) copy-start(f32[256,512]{1,0:T(8,128)} %get-tuple-element.91.refs_6_) | copy-start | bytes 1572868
  74.9 4.2 %collective-permute-start.9 = (f32[256,1536]{1,0:T(8,128)S(1)}, f32[256,1536]{1,0:T(8,128)S(1)}, u32[]{:S(2)}, u32[]{:S(2)}) collective-permute-start(f32[256,1536]{1,0:T(8,128)S(1)} %get-tuple-element.109), channel_id=1, source_target_pairs={{0,1},{1,0},{2,3},{3,2},{4,5},{5,4},{6,7},{7,6},{8,9},{9,8},{10,11... | collective-permute-start | bytes 4718600 | tf_op jit(solution)/shard_map/ppermute | solution.py:34
  75.0 4.1 %collective-permute-start.8 = (f32[256,512]{1,0:T(8,128)S(1)}, f32[256,512]{1,0:T(8,128)S(1)}, u32[]{:S(2)}, u32[]{:S(2)}) collective-permute-start(f32[256,512]{1,0:T(8,128)S(1)} %get-tuple-element.108), channel_id=1, source_target_pairs={{0,1},{1,0},{2,3},{3,2},{4,5},{5,4},{6,7},{7,6},{8,9},{9,8},{10,11... | collective-permute-start | bytes 1572872 | tf_op jit(solution)/shard_map/ppermute | solution.py:34
  79.2 10.3 %copy-start.12 = (f32[256,512]{1,0:T(8,128)S(1)}, f32[256,512]{1,0:T(8,128)}, u32[]{:S(2)}) copy-start(f32[256,512]{1,0:T(8,128)} %get-tuple-element.106.refs_5_) | copy-start | bytes 1572868
  79.2 10.3 %copy-start.13 = (f32[256,512]{1,0:T(8,128)S(1)}, f32[256,512]{1,0:T(8,128)}, u32[]{:S(2)}) copy-start(f32[256,512]{1,0:T(8,128)} %get-tuple-element.107.refs_6_) | copy-start | bytes 1572868
  79.9 28.7 %collective-permute-start.11 = (f32[128,2048]{1,0:T(8,128)S(1)}, f32[128,2048]{1,0:T(8,128)S(1)}, u32[]{:S(2)}, u32[]{:S(2)}) collective-permute-start(f32[128,2048]{1,0:T(8,128)S(1)} %get-tuple-element.116), channel_id=1, source_target_pairs={{0,8},{1,9},{2,10},{3,11},{4,12},{5,13},{6,14},{7,15},{8,0},{9,1},... | collective-permute-start | bytes 3145736 | tf_op jit(solution)/shard_map/ppermute | solution.py:34
  94.5 15.7 %collective-permute-start.10 = (f32[256,1536]{1,0:T(8,128)S(1)}, f32[256,1536]{1,0:T(8,128)S(1)}, u32[]{:S(2)}, u32[]{:S(2)}) collective-permute-start(f32[256,1536]{1,0:T(8,128)S(1)} %get-tuple-element.115), channel_id=1, source_target_pairs={{0,1},{1,0},{2,3},{3,2},{4,5},{5,4},{6,7},{7,6},{8,9},{9,8},{10,11... | collective-permute-start | bytes 4718600 | tf_op jit(solution)/shard_map/ppermute | solution.py:34
  94.6 21.7 %collective-permute-start.12 = (f32[256,512]{1,0:T(8,128)S(1)}, f32[256,512]{1,0:T(8,128)S(1)}, u32[]{:S(2)}, u32[]{:S(2)}) collective-permute-start(f32[256,512]{1,0:T(8,128)S(1)} %get-tuple-element.103.refs_5_.refs_1_), channel_id=1, source_target_pairs={{0,1},{1,0},{2,3},{3,2},{4,5},{5,4},{6,7},{7,6},{8,9},{9,8},{10,11... | collective-permute-start | bytes 1572872 | tf_op jit(solution)/shard_map/ppermute | solution.py:29
  95.1 23.9 %collective-permute-start.13 = (f32[256,512]{1,0:T(8,128)S(1)}, f32[256,512]{1,0:T(8,128)S(1)}, u32[]{:S(2)}, u32[]{:S(2)}) collective-permute-start(f32[256,512]{1,0:T(8,128)S(1)} %get-tuple-element.103.refs_5_.refs_1_), channel_id=1, source_target_pairs={{1,2},{2,1},{3,4},{4,3},{5,6},{6,5},{7,8},{8,7},{9,10},{10,9},{11,... | collective-permute-start | bytes 1572872 | tf_op jit(solution)/shard_map/ppermute | solution.py:29
  95.8 25.2 %collective-permute-start.14 = (f32[256,512]{1,0:T(8,128)S(1)}, f32[256,512]{1,0:T(8,128)S(1)}, u32[]{:S(2)}, u32[]{:S(2)}) collective-permute-start(f32[256,512]{1,0:T(8,128)S(1)} %get-tuple-element.111.refs_6_.refs_1_), channel_id=1, source_target_pairs={{0,1},{1,0},{2,3},{3,2},{4,5},{5,4},{6,7},{7,6},{8,9},{9,8},{10,11... | collective-permute-start | bytes 1572872 | tf_op jit(solution)/shard_map/ppermute | solution.py:29
  108.6 13.9 %collective-permute-start.15 = (f32[256,512]{1,0:T(8,128)S(1)}, f32[256,512]{1,0:T(8,128)S(1)}, u32[]{:S(2)}, u32[]{:S(2)}) collective-permute-start(f32[256,512]{1,0:T(8,128)S(1)} %get-tuple-element.111.refs_6_.refs_1_), channel_id=1, source_target_pairs={{1,2},{2,1},{3,4},{4,3},{5,6},{6,5},{7,8},{8,7},{9,10},{10,9},{11,... | collective-permute-start | bytes 1572872 | tf_op jit(solution)/shard_map/ppermute | solution.py:29
  110.9 30.7 %collective-permute-start.16 = (f32[128,1536]{1,0:T(8,128)S(1)}, f32[128,1536]{1,0:T(8,128)S(1)}, u32[]{:S(2)}, u32[]{:S(2)}) collective-permute-start(f32[128,1536]{1,0:T(8,128)S(1)} %get-tuple-element.120), channel_id=1, source_target_pairs={{0,2},{1,3},{2,0},{3,1},{4,6},{5,7},{6,4},{7,5},{8,10},{9,11},{10,... | collective-permute-start | bytes 2359304 | tf_op jit(solution)/shard_map/ppermute | solution.py:34
  116.3 28.1 %collective-permute-start.19 = (f32[32,2048]{1,0:T(8,128)S(1)}, f32[32,2048]{1,0:T(8,128)S(1)}, u32[]{:S(2)}, u32[]{:S(2)}) collective-permute-start(f32[32,2048]{1,0:T(8,128)S(1)} %get-tuple-element.125), channel_id=1, source_target_pairs={{0,16},{1,17},{2,18},{3,19},{4,20},{5,21},{6,22},{7,23},{8,24},{9,... | collective-permute-start | bytes 786440 | tf_op jit(solution)/shard_map/ppermute | solution.py:34
  119.0 25.5 %collective-permute-start.20 = (f32[32,2048]{1,0:T(8,128)S(1)}, f32[32,2048]{1,0:T(8,128)S(1)}, u32[]{:S(2)}, u32[]{:S(2)}) collective-permute-start(f32[32,2048]{1,0:T(8,128)S(1)} %get-tuple-element.126), channel_id=1, source_target_pairs={{0,4},{1,5},{2,6},{3,7},{4,0},{5,1},{6,2},{7,3},{8,12},{9,13},{10,... | collective-permute-start | bytes 786440 | tf_op jit(solution)/shard_map/ppermute | solution.py:34
  119.4 3.1 %copy-start.11 = (f32[512,512]{1,0:T(8,128)S(1)}, f32[512,512]{1,0:T(8,128)}, u32[]{:S(2)}) copy-start(f32[512,512]{1,0:T(8,128)} %copy-done.10) | copy-start | bytes 3145732
  121.0 23.4 %collective-permute-start.21 = (f32[32,2048]{1,0:T(8,128)S(1)}, f32[32,2048]{1,0:T(8,128)S(1)}, u32[]{:S(2)}, u32[]{:S(2)}) collective-permute-start(f32[32,2048]{1,0:T(8,128)S(1)} %get-tuple-element.127), channel_id=1, source_target_pairs={{0,20},{1,21},{2,22},{3,23},{4,16},{5,17},{6,18},{7,19},{8,28},{9,... | collective-permute-start | bytes 786440 | tf_op jit(solution)/shard_map/ppermute | solution.py:34
  124.9 20.8 %collective-permute-start.18 = (f32[256,1024]{1,0:T(8,128)S(1)}, f32[256,1024]{1,0:T(8,128)S(1)}, u32[]{:S(2)}, u32[]{:S(2)}) collective-permute-start(f32[256,1024]{1,0:T(8,128)S(1)} %get-tuple-element.124), channel_id=1, source_target_pairs={{0,1},{1,0},{2,3},{3,2},{4,5},{5,4},{6,7},{7,6},{8,9},{9,8},{10,11... | collective-permute-start | bytes 3145736 | tf_op jit(solution)/shard_map/ppermute | solution.py:34
  142.2 11.6 %collective-permute-start.17 = (f32[64,1536]{1,0:T(8,128)S(1)}, f32[64,1536]{1,0:T(8,128)S(1)}, u32[]{:S(2)}, u32[]{:S(2)}) collective-permute-start(f32[64,1536]{1,0:T(8,128)S(1)} %get-tuple-element.123), channel_id=1, source_target_pairs={{0,8},{1,9},{2,10},{3,11},{4,12},{5,13},{6,14},{7,15},{8,0},{9,1},... | collective-permute-start | bytes 1179656 | tf_op jit(solution)/shard_map/ppermute | solution.py:34
  145.1 6.1 %collective-permute-start.30 = (f32[16,2048]{1,0:T(8,128)S(1)}, f32[16,2048]{1,0:T(8,128)S(1)}, u32[]{:S(2)}, u32[]{:S(2)}) collective-permute-start(f32[16,2048]{1,0:T(8,128)S(1)} %get-tuple-element.141), channel_id=1, source_target_pairs={{0,2},{1,3},{2,0},{3,1},{4,6},{5,7},{6,4},{7,5},{8,10},{9,11},{10,... | collective-permute-start | bytes 393224 | tf_op jit(solution)/shard_map/ppermute | solution.py:34
  146.4 11.9 %collective-permute-start.22 = (f32[64,1024]{1,0:T(8,128)S(1)}, f32[64,1024]{1,0:T(8,128)S(1)}, u32[]{:S(2)}, u32[]{:S(2)}) collective-permute-start(f32[64,1024]{1,0:T(8,128)S(1)} %get-tuple-element.131), channel_id=1, source_target_pairs={{0,4},{1,5},{2,6},{3,7},{4,0},{5,1},{6,2},{7,3},{8,12},{9,13},{10,... | collective-permute-start | bytes 786440 | tf_op jit(solution)/shard_map/ppermute | solution.py:34
  147.7 10.6 %collective-permute-start.23 = (f32[64,1024]{1,0:T(8,128)S(1)}, f32[64,1024]{1,0:T(8,128)S(1)}, u32[]{:S(2)}, u32[]{:S(2)}) collective-permute-start(f32[64,1024]{1,0:T(8,128)S(1)} %get-tuple-element.132), channel_id=1, source_target_pairs={{0,2},{1,3},{2,0},{3,1},{4,6},{5,7},{6,4},{7,5},{8,10},{9,11},{10,... | collective-permute-start | bytes 786440 | tf_op jit(solution)/shard_map/ppermute | solution.py:34
  149.7 12.9 %collective-permute-start.24 = (f32[64,1024]{1,0:T(8,128)S(1)}, f32[64,1024]{1,0:T(8,128)S(1)}, u32[]{:S(2)}, u32[]{:S(2)}) collective-permute-start(f32[64,1024]{1,0:T(8,128)S(1)} %get-tuple-element.133), channel_id=1, source_target_pairs={{0,6},{1,7},{2,4},{3,5},{4,2},{5,3},{6,0},{7,1},{8,14},{9,15},{10,... | collective-permute-start | bytes 786440 | tf_op jit(solution)/shard_map/ppermute | solution.py:34
  154.4 14.3 %collective-permute-start.28 = (f32[32,1536]{1,0:T(8,128)S(1)}, f32[32,1536]{1,0:T(8,128)S(1)}, u32[]{:S(2)}, u32[]{:S(2)}) collective-permute-start(f32[32,1536]{1,0:T(8,128)S(1)} %get-tuple-element.138), channel_id=1, source_target_pairs={{0,16},{1,17},{2,18},{3,19},{4,20},{5,21},{6,22},{7,23},{8,24},{9,... | collective-permute-start | bytes 589832 | tf_op jit(solution)/shard_map/ppermute | solution.py:34
  163.2 6.9 %collective-permute-start.25 = (f32[16,1024]{1,0:T(8,128)S(1)}, f32[16,1024]{1,0:T(8,128)S(1)}, u32[]{:S(2)}, u32[]{:S(2)}) collective-permute-start(f32[16,1024]{1,0:T(8,128)S(1)} %get-tuple-element.135), channel_id=1, source_target_pairs={{0,16},{1,17},{2,18},{3,19},{4,20},{5,21},{6,22},{7,23},{8,24},{9,... | collective-permute-start | bytes 196616 | tf_op jit(solution)/shard_map/ppermute | solution.py:34
  163.5 6.6 %collective-permute-start.26 = (f32[16,1024]{1,0:T(8,128)S(1)}, f32[16,1024]{1,0:T(8,128)S(1)}, u32[]{:S(2)}, u32[]{:S(2)}) collective-permute-start(f32[16,1024]{1,0:T(8,128)S(1)} %get-tuple-element.136), channel_id=1, source_target_pairs={{0,8},{1,9},{2,10},{3,11},{4,12},{5,13},{6,14},{7,15},{8,0},{9,1},... | collective-permute-start | bytes 196616 | tf_op jit(solution)/shard_map/ppermute | solution.py:34
  165.6 6.1 %collective-permute-start.27 = (f32[16,1024]{1,0:T(8,128)S(1)}, f32[16,1024]{1,0:T(8,128)S(1)}, u32[]{:S(2)}, u32[]{:S(2)}) collective-permute-start(f32[16,1024]{1,0:T(8,128)S(1)} %get-tuple-element.137), channel_id=1, source_target_pairs={{0,24},{1,25},{2,26},{3,27},{4,28},{5,29},{6,30},{7,31},{8,16},{9,... | collective-permute-start | bytes 196616 | tf_op jit(solution)/shard_map/ppermute | solution.py:34
  169.3 4.7 %collective-permute-start.29 = (f32[16,1536]{1,0:T(8,128)S(1)}, f32[16,1536]{1,0:T(8,128)S(1)}, u32[]{:S(2)}, u32[]{:S(2)}) collective-permute-start(f32[16,1536]{1,0:T(8,128)S(1)} %get-tuple-element.140), channel_id=1, source_target_pairs={{0,4},{1,5},{2,6},{3,7},{4,0},{5,1},{6,2},{7,3},{8,12},{9,13},{10,... | collective-permute-start | bytes 294920 | tf_op jit(solution)/shard_map/ppermute | solution.py:34
